TPU v7x, 768 devices: a whole 4x8x12 slice. The times are simulated.
768 devices in a mesh: dom: 32 (over x, y), col: 24 (over z, core).
Axes of the slice: x: 4, y: 8, z: 12, core: 2. Of those that a mesh axis runs over, the one named last changes fastest.
Arguments:
- a_tiles: bfloat16 [64, 96, 12, 128, 128], P('dom', 'col'), may hold values from -6 to 6
- p_tiles: bfloat16 [64, 96, 128, 128], P('dom', 'col'), may hold values from -0.1875 to 0.1875
- a_cols: int32 [64, 96, 12], P('dom', 'col'), may hold values from -1 to 6143, as said below
- slot_map: int32 [64, 96, 12], P('dom', 'col'), may hold values from 0 to 3
- aggregate: int32 [64, 96], P('dom', 'col'), may hold values from 0 to 767, as said below
Outputs:
- coarse_tiles: float32 [32, 24, 4, 128, 128], P('dom', 'col')
Inputs may be any that keep to these rules, and one draw needn't show every extreme that they name: `a_cols`: slot 0 of fine tile (x, y) names the tile itself; the other slots name distinct tiles (x', y') with |x' - x| <= 2 and |y' - y| <= 2 inside the grid, or hold -1. `aggregate`: for fine tile (x, y) the coarse tile a * 24 + b has a = x // 2 and b within one of y // 4.
All inputs are finite; a program needn't handle non-finite values.
Results may differ from a plain program's by a relative error of at most 0.0029.
Values may be sent and summed in bfloat16 or wider, within the bound.
A program may use at most 32 MiB of HBM per device.

v0:
```python
import jax
import jax.numpy as jnp
from jax import lax
from jax.sharding import PartitionSpec as P

CSLOTS = 4


def extended(block, sides, width):
    for axis, dim in sides:
        count = lax.axis_size(axis)
        forward = [(i, i + 1) for i in range(count - 1)]
        backward = [(target, source) for source, target in forward]
        low = lax.ppermute(
            lax.slice_in_dim(block, block.shape[dim] - width, None, axis=dim), axis, forward
        )
        high = lax.ppermute(lax.slice_in_dim(block, 0, width, axis=dim), axis, backward)
        block = jnp.concatenate([low, block, high], axis=dim)
    return block


def shifted(value, axis, steps):
    count = lax.axis_size(axis)
    first, last = (max(0, -steps), min(count, count - steps))
    return lax.ppermute(value, axis, [(source, source + steps) for source in range(first, last)])


def body(a_tiles, p_tiles, a_cols, slot_map, aggregate):
    rows_x, rows_y, slot_count = a_cols.shape
    tile_rows = p_tiles.shape[2]
    coarse_width = p_tiles.shape[3]
    col_count = lax.axis_size("col")
    col_here = lax.axis_index("col")
    first_x = lax.axis_index("dom") * rows_x
    first_y = col_here * rows_y
    width_y = rows_y * col_count
    padded = extended(p_tiles, (("dom", 0), ("col", 1)), 2)
    is_live = a_cols >= 0
    near_x = a_cols // width_y - first_x + 2
    near_y = a_cols % width_y - first_y + 2
    flat_index = jnp.where(is_live, near_x * (rows_y + 4) + near_y, 0)
    ghosts = padded.reshape(-1, tile_rows, coarse_width)[flat_index]
    product = jnp.einsum(
        "xykab,xykbc->xykac", a_tiles, ghosts, preferred_element_type=jnp.float32
    ).astype(jnp.bfloat16)
    slot_select = (
        (slot_map[..., None] == jnp.arange(CSLOTS, dtype=jnp.int32)) & is_live[..., None]
    ).astype(jnp.bfloat16)
    slot_sums = jnp.einsum(
        "xykj,xykac->xyjac", slot_select, product, preferred_element_type=jnp.float32
    )
    terms = jnp.einsum(
        "xyba,xyjbc->xyjac", p_tiles.astype(jnp.float32), slot_sums, precision=lax.Precision.HIGHEST
    )
    side_index = aggregate % col_count - col_here + 1
    side_select = (side_index[..., None] == jnp.arange(3, dtype=jnp.int32)).astype(jnp.float32)
    buckets = jnp.einsum("xys,xyjac->sjac", side_select, terms, precision=lax.Precision.HIGHEST)
    from_left = shifted(buckets[2], "col", 1)
    from_right = shifted(buckets[0], "col", -1)
    result = buckets[1] + from_left + from_right
    return result[None, None]


def solution(mesh):
    in_specs = (
        P("dom", "col", None, None, None),
        P("dom", "col", None, None),
        P("dom", "col", None),
        P("dom", "col", None),
        P("dom", "col"),
    )
    out_specs = P("dom", "col", None, None, None)
    return jax.shard_map(body, mesh=mesh, in_specs=in_specs, out_specs=out_specs, check_vma=False)
```

profile of v0, /device:TPU:219, one launch (start us, length us, event | category | flops | bytes accessed | tf_op | source)
XLA Modules:
  0.0 75.9 jit_solution(16055190742773312960)
XLA Ops:
  0.0 0.0 copy-start
  0.0 4.7 %collective-permute-start = (bf16[2,4,128,128]{3,2,1,0:T(8,128)(2,1)}, bf16[2,4,128,128]{3,2,1,0:T(8,128)(2,1)}, u32[]{:S(2)}, u32[]{:S(2)}) collective-permute-start(bf16[2,4,128,128]{3,2,1,0:T(8,128)(2,1)} %param.6), channel_id=1, source_target_pairs={{0,24},{24,48},{48,72},{72,96},{96,120},{120,144},{144,168},{168,1... | collective-permute-start | bytes 786440 | tf_op jit(solution)/shard_map/ppermute | solution.py:14
  4.7 1.9 %collective-permute-start.1 = (bf16[2,4,128,128]{3,2,1,0:T(8,128)(2,1)}, bf16[2,4,128,128]{3,2,1,0:T(8,128)(2,1)S(1)}, u32[]{:S(2)}, u32[]{:S(2)}) collective-permute-start(bf16[2,4,128,128]{3,2,1,0:T(8,128)(2,1)} %param.6), channel_id=1, source_target_pairs={{24,0},{48,24},{72,48},{96,72},{120,96},{144,120},{168,144},{192,1... | collective-permute-start | bytes 786440 | tf_op jit(solution)/shard_map/ppermute | solution.py:17
  6.6 0.7 compare_select_fusion
  7.4 0.1 reshape.9
  7.4 2.5 %collective-permute-done = bf16[2,4,128,128]{3,2,1,0:T(8,128)(2,1)} collective-permute-done((bf16[2,4,128,128]{3,2,1,0:T(8,128)(2,1)}, bf16[2,4,128,128]{3,2,1,0:T(8,128)(2,1)}, u32[]{:S(2)}, u32[]{:S(2)}) %collective-permute-start) | collective-permute-done | bytes 262176 | tf_op jit(solution)/shard_map/ppermute | solution.py:14
  10.0 1.0 %constant_dynamic-update-slice_fusion.2 = bf16[6,4,128,128]{3,2,1,0:T(8,128)(2,1)S(1)} fusion(bf16[2,4,128,128]{3,2,1,0:T(8,128)(2,1)} %collective-permute-done), kind=kLoop, calls=%fused_computation.19 | loop fusion | bytes 524288
  10.9 1.0 %constant_dynamic-update-slice_fusion.1 = bf16[6,4,128,128]{3,2,1,0:T(8,128)(2,1)S(1)} fusion(bf16[6,4,128,128]{3,2,1,0:T(8,128)(2,1)S(1)} %constant_dynamic-update-slice_fusion.2, bf16[2,4,128,128]{3,2,1,0:T(8,128)(2,1)} %param.6), kind=kLoop, calls=%fused_computation.18 | loop fusion | bytes 524288
  11.9 2.9 %collective-permute-done.1 = bf16[2,4,128,128]{3,2,1,0:T(8,128)(2,1)S(1)} collective-permute-done((bf16[2,4,128,128]{3,2,1,0:T(8,128)(2,1)}, bf16[2,4,128,128]{3,2,1,0:T(8,128)(2,1)S(1)}, u32[]{:S(2)}, u32[]{:S(2)}) %collective-permute-start.1) | collective-permute-done | bytes 262176 | tf_op jit(solution)/shard_map/ppermute | solution.py:17
  14.9 0.1 fusion.25
  15.0 7.0 %collective-permute-start.2 = (bf16[6,2,128,128]{3,2,1,0:T(8,128)(2,1)S(1)}, bf16[6,2,128,128]{3,2,1,0:T(8,128)(2,1)S(1)}, u32[]{:S(2)}, u32[]{:S(2)}) collective-permute-start(bf16[6,2,128,128]{3,2,1,0:T(8,128)(2,1)S(1)} %get-tuple-element.8), channel_id=1, source_target_pairs={{0,1},{1,2},{2,3},{3,4},{4,5},{5,6},{6,7},{7,8},{8,9},{9,10},{10,1... | collective-permute-start | bytes 1179656 | tf_op jit(solution)/shard_map/ppermute | solution.py:14
  21.9 1.9 %collective-permute-start.3 = (bf16[6,2,128,128]{3,2,1,0:T(8,128)(2,1)S(1)}, bf16[6,2,128,128]{3,2,1,0:T(8,128)(2,1)S(1)}, u32[]{:S(2)}, u32[]{:S(2)}) collective-permute-start(bf16[6,2,128,128]{3,2,1,0:T(8,128)(2,1)S(1)} %get-tuple-element.9), channel_id=1, source_target_pairs={{1,0},{2,1},{3,2},{4,3},{5,4},{6,5},{7,6},{8,7},{9,8},{10,9},{11,1... | collective-permute-start | bytes 1179656 | tf_op jit(solution)/shard_map/ppermute | solution.py:17
  23.9 0.0 copy-done.4
  23.9 0.0 copy-done.2
  23.9 2.7 %collective-permute-done.2 = bf16[6,2,128,128]{3,2,1,0:T(8,128)(2,1)S(1)} collective-permute-done((bf16[6,2,128,128]{3,2,1,0:T(8,128)(2,1)S(1)}, bf16[6,2,128,128]{3,2,1,0:T(8,128)(2,1)S(1)}, u32[]{:S(2)}, u32[]{:S(2)}) %collective-permute-start.2) | collective-permute-done | bytes 393248 | tf_op jit(solution)/shard_map/ppermute | solution.py:14
  26.6 5.6 %collective-permute-done.3 = bf16[6,2,128,128]{3,2,1,0:T(8,128)(2,1)S(1)} collective-permute-done((bf16[6,2,128,128]{3,2,1,0:T(8,128)(2,1)S(1)}, bf16[6,2,128,128]{3,2,1,0:T(8,128)(2,1)S(1)}, u32[]{:S(2)}, u32[]{:S(2)}) %collective-permute-start.3) | collective-permute-done | bytes 393248 | tf_op jit(solution)/shard_map/ppermute | solution.py:17
  32.2 1.3 %pad_maximum_fusion = bf16[6,8,128,128]{3,2,1,0:T(8,128)(2,1)} fusion(bf16[6,2,128,128]{3,2,1,0:T(8,128)(2,1)S(1)} %collective-permute-done.3, bf16[6,4,128,128]{3,2,1,0:T(8,128)(2,1)S(1)} %constant_dynamic-update-slice_fusion, bf16[6,2,128,128]{3,2,1,0:T(8,128)(2,1)S(1)} %collective-permute-done.2), kind=kLoop, calls=%fused_computation.6 | loop fusion | flops 1572864 | bytes 3145728 | tf_op jit(solution)/shard_map/concatenate | solution.py:18
  33.6 4.1 %gather_fusion = bf16[96,128,128]{2,1,0:T(8,128)(2,1)} fusion(bf16[48,128,128]{2,1,0:T(8,128)(2,1)} %bitcast.39, s32[1024]{0:T(1024)S(1)} %pad_clamp_fusion), kind=kCustom, calls=%fused_computation | custom fusion | bytes 6291840 | tf_op jit(solution)/shard_map/gather | solution.py:42
  37.7 0.0 copy-done
  37.7 5.9 %convert_bitcast_fusion = bf16[2,4,12,128,128]{3,4,2,1,0:T(8,128)(2,1)} fusion(bf16[2,4,12,128,128]{4,3,2,1,0:T(8,128)(2,1)} %bitcast.40, bf16[2,4,12,128,128]{4,3,2,1,0:T(8,128)(2,1)S(1)} %copy-done), kind=kOutput, calls=%fused_computation.1 | convolution fusion | flops 404226048 | bytes 9437184 | tf_op jit(solution)/shard_map/xykab,xykbc->xykac/dot_general | solution.py:43
  43.6 7.6 %copy.9 = bf16[2,4,12,128,128]{4,2,3,1,0:T(8,128)(2,1)} copy(bf16[2,4,12,128,128]{3,4,2,1,0:T(8,128)(2,1)} %convert_bitcast_fusion) | data formatting | bytes 6291456 | tf_op jit(solution)/shard_map/convert_element_type | solution.py:45
  51.2 0.0 copy-done.3
  51.2 3.1 %fusion.10 = f32[2,4,4,128,128]{4,2,3,1,0:T(4,128)S(1)} fusion(bf16[2,4,12,128,128]{4,2,3,1,0:T(8,128)(2,1)} %copy.9, s32[2,4,12]{2,1,0:T(4,128)S(1)} %copy-done.3, pred[2,4,12]{2,1,0:T(4,128)(4,1)S(1)} %broadcast_compare_fusion), kind=kOutput, calls=%fused_computation.13 | convolution fusion | flops 12583680 | bytes 5243360 | tf_op jit(solution)/shard_map/xykj,xykac->xyjac/dot_general | solution.py:49
  54.3 3.1 %fusion.2 = f32[2,4,4,128,128]{4,3,2,1,0:T(8,128)} fusion(f32[2,4,4,128,128]{4,2,3,1,0:T(4,128)S(1)} %fusion.10, bf16[2,4,128,128]{3,2,1,0:T(8,128)(2,1)S(1)} %copy-done.1), kind=kOutput, calls=%fused_computation.4 | convolution fusion | flops 805306368 | bytes 4456448 | tf_op jit(solution)/shard_map/xyba,xyjbc->xyjac/dot_general | solution.py:52
  57.4 2.9 %copy.12 = f32[2,4,4,128,128]{3,1,0,4,2:T(4,128)} copy(f32[2,4,4,128,128]{4,3,2,1,0:T(8,128)} %fusion.2) | data formatting | bytes 4194304 | tf_op jit(solution)/shard_map/xyba,xyjbc->xyjac/dot_general | solution.py:52
  60.3 3.4 %fusion.4 = f32[3,4,128,128]{3,0,2,1:T(4,128)S(1)} fusion(f32[2,4,4,128,128]{3,1,0,4,2:T(4,128)} %copy.12, s32[2,4]{1,0:T(2,128)S(1)} %fusion.23), kind=kOutput, calls=%fused_computation.7 | convolution fusion | flops 18874392 | bytes 2883616 | tf_op jit(solution)/shard_map/xys,xyjac->sjac/dot_general | solution.py:57
  63.7 0.6 fusion.24
  64.3 1.9 %collective-permute-start.4 = (f32[4,128,128]{2,1,0:T(8,128)S(1)}, f32[4,128,128]{2,1,0:T(8,128)S(1)}, u32[]{:S(2)}, u32[]{:S(2)}) collective-permute-start(f32[4,128,128]{2,1,0:T(8,128)S(1)} %bitcast.43), channel_id=1, source_target_pairs={{0,1},{1,2},{2,3},{3,4},{4,5},{5,6},{6,7},{7,8},{8,9},{9,10},{10,1... | collective-permute-start | bytes 786440 | tf_op jit(solution)/shard_map/ppermute | solution.py:25
  66.3 2.4 %collective-permute-start.5 = (f32[4,128,128]{2,1,0:T(8,128)S(1)}, f32[4,128,128]{2,1,0:T(8,128)S(1)}, u32[]{:S(2)}, u32[]{:S(2)}) collective-permute-start(f32[4,128,128]{2,1,0:T(8,128)S(1)} %bitcast.42), channel_id=1, source_target_pairs={{1,0},{2,1},{3,2},{4,3},{5,4},{6,5},{7,6},{8,7},{9,8},{10,9},{11,1... | collective-permute-start | bytes 786440 | tf_op jit(solution)/shard_map/ppermute | solution.py:25
  68.7 0.9 %collective-permute-done.4 = f32[4,128,128]{2,1,0:T(8,128)S(1)} collective-permute-done((f32[4,128,128]{2,1,0:T(8,128)S(1)}, f32[4,128,128]{2,1,0:T(8,128)S(1)}, u32[]{:S(2)}, u32[]{:S(2)}) %collective-permute-start.4) | collective-permute-done | bytes 262176 | tf_op jit(solution)/shard_map/ppermute | solution.py:25
  69.6 5.6 %collective-permute-done.5 = f32[4,128,128]{2,1,0:T(8,128)S(1)} collective-permute-done((f32[4,128,128]{2,1,0:T(8,128)S(1)}, f32[4,128,128]{2,1,0:T(8,128)S(1)}, u32[]{:S(2)}, u32[]{:S(2)}) %collective-permute-start.5) | collective-permute-done | bytes 262176 | tf_op jit(solution)/shard_map/ppermute | solution.py:25
  75.2 0.8 add_bitcast_fusion
  (9 shorter events, 0.1 us)
Async XLA Ops:
  0.0 37.7 %copy-start = (bf16[2,4,12,128,128]{4,3,2,1,0:T(8,128)(2,1)S(1)}, bf16[2,4,12,128,128]{4,3,2,1,0:T(8,128)(2,1)}, u32[]{:S(2)}) copy-start(bf16[2,4,12,128,128]{4,3,2,1,0:T(8,128)(2,1)} %param.5) | copy-start | bytes 9437188
  0.0 23.9 %copy-start.2 = (s32[2,4,12]{2,1,0:T(4,128)S(1)}, s32[2,4,12]{2,1,0:T(4,128)}, u32[]{:S(2)}) copy-start(s32[2,4,12]{2,1,0:T(4,128)} %param.7) | copy-start | bytes 1156
  0.0 23.9 %copy-start.4 = (s32[2,4]{1,0:T(2,128)S(1)}, s32[2,4]{1,0:T(2,128)}, u32[]{:S(2)}) copy-start(s32[2,4]{1,0:T(2,128)} %param.9) | copy-start | bytes 100
  0.0 10.0 %collective-permute-start = (bf16[2,4,128,128]{3,2,1,0:T(8,128)(2,1)}, bf16[2,4,128,128]{3,2,1,0:T(8,128)(2,1)}, u32[]{:S(2)}, u32[]{:S(2)}) collective-permute-start(bf16[2,4,128,128]{3,2,1,0:T(8,128)(2,1)} %param.6), channel_id=1, source_target_pairs={{0,24},{24,48},{48,72},{72,96},{96,120},{120,144},{144,168},{168,1... | collective-permute-start | bytes 786440 | tf_op jit(solution)/shard_map/ppermute | solution.py:14
  4.7 10.2 %collective-permute-start.1 = (bf16[2,4,128,128]{3,2,1,0:T(8,128)(2,1)}, bf16[2,4,128,128]{3,2,1,0:T(8,128)(2,1)S(1)}, u32[]{:S(2)}, u32[]{:S(2)}) collective-permute-start(bf16[2,4,128,128]{3,2,1,0:T(8,128)(2,1)} %param.6), channel_id=1, source_target_pairs={{24,0},{48,24},{72,48},{96,72},{120,96},{144,120},{168,144},{192,1... | collective-permute-start | bytes 786440 | tf_op jit(solution)/shard_map/ppermute | solution.py:17
  15.0 11.7 %collective-permute-start.2 = (bf16[6,2,128,128]{3,2,1,0:T(8,128)(2,1)S(1)}, bf16[6,2,128,128]{3,2,1,0:T(8,128)(2,1)S(1)}, u32[]{:S(2)}, u32[]{:S(2)}) collective-permute-start(bf16[6,2,128,128]{3,2,1,0:T(8,128)(2,1)S(1)} %get-tuple-element.8), channel_id=1, source_target_pairs={{0,1},{1,2},{2,3},{3,4},{4,5},{5,6},{6,7},{7,8},{8,9},{9,10},{10,1... | collective-permute-start | bytes 1179656 | tf_op jit(solution)/shard_map/ppermute | solution.py:14
  21.9 10.3 %collective-permute-start.3 = (bf16[6,2,128,128]{3,2,1,0:T(8,128)(2,1)S(1)}, bf16[6,2,128,128]{3,2,1,0:T(8,128)(2,1)S(1)}, u32[]{:S(2)}, u32[]{:S(2)}) collective-permute-start(bf16[6,2,128,128]{3,2,1,0:T(8,128)(2,1)S(1)} %get-tuple-element.9), channel_id=1, source_target_pairs={{1,0},{2,1},{3,2},{4,3},{5,4},{6,5},{7,6},{8,7},{9,8},{10,9},{11,1... | collective-permute-start | bytes 1179656 | tf_op jit(solution)/shard_map/ppermute | solution.py:17
  43.6 7.6 %copy-start.3 = (s32[2,4,12]{2,1,0:T(4,128)S(1)}, s32[2,4,12]{2,1,0:T(4,128)}, u32[]{:S(2)}) copy-start(s32[2,4,12]{2,1,0:T(4,128)} %param.8) | copy-start | bytes 1156
  51.2 3.1 %copy-start.1 = (bf16[2,4,128,128]{3,2,1,0:T(8,128)(2,1)S(1)}, bf16[2,4,128,128]{3,2,1,0:T(8,128)(2,1)}, u32[]{:S(2)}) copy-start(bf16[2,4,128,128]{3,2,1,0:T(8,128)(2,1)} %param.6) | copy-start | bytes 786436
  64.3 5.2 %collective-permute-start.4 = (f32[4,128,128]{2,1,0:T(8,128)S(1)}, f32[4,128,128]{2,1,0:T(8,128)S(1)}, u32[]{:S(2)}, u32[]{:S(2)}) collective-permute-start(f32[4,128,128]{2,1,0:T(8,128)S(1)} %bitcast.43), channel_id=1, source_target_pairs={{0,1},{1,2},{2,3},{3,4},{4,5},{5,6},{6,7},{7,8},{8,9},{9,10},{10,1... | collective-permute-start | bytes 786440 | tf_op jit(solution)/shard_map/ppermute | solution.py:25
  66.3 8.9 %collective-permute-start.5 = (f32[4,128,128]{2,1,0:T(8,128)S(1)}, f32[4,128,128]{2,1,0:T(8,128)S(1)}, u32[]{:S(2)}, u32[]{:S(2)}) collective-permute-start(f32[4,128,128]{2,1,0:T(8,128)S(1)} %bitcast.42), channel_id=1, source_target_pairs={{1,0},{2,1},{3,2},{4,3},{5,4},{6,5},{7,6},{8,7},{9,8},{10,9},{11,1... | collective-permute-start | bytes 786440 | tf_op jit(solution)/shard_map/ppermute | solution.py:25
where the time goes:
time: 76.5 us; the launch traced here: 75.9 us
  waiting for transfers between devices  20.3 us (27%)
  starting transfers between devices  19.8 us (26%)
  local copies, waits for them, and re-layouts  17.4 us (23%)
  matrix products  15.5 us (20%)
  other arithmetic  2.81 us (4%)
    ppermute x2, starting transfers between devices, extended(): lax.ppermute(lax.slice_in_dim(block, block.shape[dim] - width, None, axis...  11.6 us
    ppermute x2, waiting for transfers between devices, extended(): lax.ppermute(lax.slice_in_dim(block, 0, width, axis=dim), axis, backward)  8.55 us
    convert_element_type x1, local copies, waits for them, and re-layouts, body(): product = jnp.einsum('xykab,xykbc->xykac', a_tiles, ghosts, preferred_ele...  7.63 us
    ppermute x2, waiting for transfers between devices, shifted(): lax.ppermute(value, axis, [(source, source + steps) for source in range(f...  6.49 us
    dot_general x1, matrix products, body(): jnp.einsum('xykab,xykbc->xykac', a_tiles, ghosts, preferred_element_type=...  5.92 us
    ppermute x2, waiting for transfers between devices, extended(): lax.ppermute(lax.slice_in_dim(block, block.shape[dim] - width, None, axis...  5.24 us
    ppermute x2, starting transfers between devices, shifted(): lax.ppermute(value, axis, [(source, source + steps) for source in range(f...  4.33 us
    gather x1, local copies, waits for them, and re-layouts, body(): ghosts = padded.reshape(-1, tile_rows, coarse_width)[flat_index]  4.08 us
  transfers between devices with their start and end apart: 6, of which 6 were waited for; matrix products, arithmetic and copies ran while one was open for 4% of the time, Pallas kernels for 0%

commit v1 on v0

v1 whole, which is shorter than its diff:
```python
import functools

import jax
import jax.numpy as jnp
from jax import lax
from jax.experimental import pallas as pl
from jax.experimental.pallas import tpu as pltpu
from jax.sharding import PartitionSpec as P

CSLOTS = 4
SIDES = 3
PAIRS = 8
MESH = pl.DeviceIdType.MESH
F32 = jnp.float32
BF16 = jnp.bfloat16


def dot(left, right):
    return lax.dot_general(left, right, (((1,), (0,)), ((), ())), preferred_element_type=F32)


def split(value):
    high = value.astype(BF16)
    return high, (value - high.astype(F32)).astype(BF16)


def kernel(
    n_dom, n_col, a_cols, slot_map, aggregate, a_hbm, p_hbm, out,
    a_tiles, halo, p_turned, sums, totals, away, arrived,
    pick_a, pick_g, ends, order, side_ends,
    local_sem, row_send, row_recv, col_send, col_recv, away_send, away_recv,
):
    rows_x, rows_y, slots = a_cols.shape
    tiles = rows_x * rows_y
    tile = p_hbm.shape[-1]
    dom, col = lax.axis_index("dom"), lax.axis_index("col")
    core = lax.rem(col, 2)
    up, down = lax.rem(dom + 1, n_dom), lax.rem(dom + n_dom - 1, n_dom)
    right, left = lax.rem(col + 1, n_col), lax.rem(col + n_col - 1, n_col)
    outer, inner = jnp.where(core == 0, left, right), jnp.where(core == 0, right, left)
    edge = (2 * core, 2 - 2 * core)
    landing = (6 - 6 * core, 6 * core)

    own_p = pltpu.make_async_copy(p_hbm, halo.at[pl.ds(2, 2), pl.ds(2, 4)], local_sem.at[0])
    own_p.start()
    own_a = pltpu.make_async_copy(a_hbm, a_tiles, local_sem.at[1])
    own_a.start()

    barrier = pltpu.get_barrier_semaphore()
    for target in ((up, col), (down, col), (dom, right), (dom, left)):
        pl.semaphore_signal(barrier, inc=1, device_id=target, device_id_type=MESH)
    pl.semaphore_wait(barrier, 4)

    def along_dom(part, way):
        columns = edge[part]
        index = part * 2 + way
        return pltpu.make_async_remote_copy(
            src_ref=p_hbm.at[:, pl.ds(columns, 2)],
            dst_ref=halo.at[pl.ds(4 * way, 2), pl.ds(2 + columns, 2)],
            send_sem=row_send.at[index],
            recv_sem=row_recv.at[index],
            device_id=((up, down)[way], col),
            device_id_type=MESH,
        )

    def along_col(part, piece):
        columns = edge[part]
        index = part * 3 + piece
        rows = pl.ds(2 * piece, 2)
        source = p_hbm.at[:, pl.ds(columns, 2)] if piece == 1 else halo.at[rows, pl.ds(2 + columns, 2)]
        return pltpu.make_async_remote_copy(
            src_ref=source,
            dst_ref=halo.at[rows, pl.ds(landing[part], 2)],
            send_sem=col_send.at[index],
            recv_sem=col_recv.at[index],
            device_id=(dom, (outer, inner)[part]),
            device_id_type=MESH,
        )

    by_row = [[along_dom(part, way) for way in range(2)] for part in range(2)]
    by_col = [[along_col(part, piece) for piece in range(3)] for part in range(2)]
    by_row[0][0].start()
    by_row[0][1].start()
    by_col[0][1].start()
    by_row[1][0].start()
    by_row[1][1].start()
    by_col[1][1].start()

    halo[6, 0] = jnp.zeros((tile, tile), BF16)
    width_y = rows_y * n_col
    origin = (dom * rows_x - 2) * width_y + col * rows_y - 2
    inverse = -(-65536 // width_y)

    def tabulate(t, carry):
        x, y = t // rows_y, lax.rem(t, rows_y)
        near, groups = [], []
        for k in range(slots):
            where = a_cols[x, y, k]
            offset = where - origin
            near.append(jnp.clip(offset - (width_y - 8) * ((offset * inverse) >> 16), 0, 47))
            groups.append(jnp.where(where >= 0, slot_map[x, y, k], CSLOTS))
        begin = jnp.int32(0)
        places = [jnp.int32(-1)] * slots
        ends[t * (CSLOTS + 1)] = 0
        for j in range(CSLOTS):
            count = begin
            for k in range(slots):
                member = groups[k] == j
                places[k] = jnp.where(member, count, places[k])
                count = count + member.astype(jnp.int32)
            begin = (count + 1) & -2
            ends[t * (CSLOTS + 1) + j + 1] = begin >> 1
        for place in range(2 * PAIRS):
            slot, tile_g = jnp.int32(0), jnp.int32(48)
            for k in range(slots):
                here = places[k] == place
                slot = jnp.where(here, k, slot)
                tile_g = jnp.where(here, near[k], tile_g)
            pick_a[t * 2 * PAIRS + place] = t * slots + slot
            pick_g[t * 2 * PAIRS + place] = tile_g
        return carry

    lax.fori_loop(0, tiles, tabulate, 0)

    sides = [
        lax.rem(aggregate[t // rows_y, t % rows_y], n_col) - col + 1 for t in range(tiles)
    ]
    count = jnp.int32(0)
    places = [jnp.int32(0)] * tiles
    side_ends[0] = 0
    for side in range(SIDES):
        for t in range(tiles):
            member = sides[t] == side
            places[t] = jnp.where(member, count, places[t])
            count = count + member.astype(jnp.int32)
        side_ends[side + 1] = count
    for place in range(tiles):
        chosen = jnp.int32(0)
        for t in range(tiles):
            chosen = jnp.where(places[t] == place, t, chosen)
        order[place] = chosen

    own_p.wait()
    for t in range(tiles):
        turned = halo[2 + t // rows_y, 2 + t % rows_y].T
        p_turned[t] = jnp.concatenate([turned, turned], axis=1)

    for part in range(2):
        for way in range(2):
            by_row[part][way].wait_recv()
            by_col[part][2 * way].start()
    own_a.wait()
    for part in range(2):
        for piece in (1, 0, 2):
            by_col[part][piece].wait_recv()

    sums[0] = jnp.zeros((tile, tile), F32)
    totals[0] = jnp.zeros(totals.shape[1:], F32)

    def one_tile(place, carry):
        t = order[place]
        total = None
        for pair in range(PAIRS):
            first = t * 2 * PAIRS + 2 * pair
            lefts, rights = [], []
            for member in range(2):
                lefts.append(a_tiles[pick_a[first + member]])
                g = pick_g[first + member]
                rights.append(halo[g >> 3, g & 7])
            term = dot(jnp.concatenate(lefts, axis=1), jnp.concatenate(rights, axis=0))
            total = term if total is None else total + term
            sums[pair + 1] = total
        highs, lows = [], []
        for j in range(CSLOTS):
            base = t * (CSLOTS + 1) + j
            high, low = split(sums[ends[base + 1]] - sums[ends[base]])
            highs.append(high)
            lows.append(low)
        stacked = jnp.concatenate(
            [jnp.concatenate(highs, axis=1), jnp.concatenate(lows, axis=1)], axis=0
        )
        totals[place + 1] = totals[place] + dot(p_turned[t], stacked)
        return carry

    lax.fori_loop(0, tiles, one_tile, 0)

    def leaving(way):
        return pltpu.make_async_remote_copy(
            src_ref=away.at[way],
            dst_ref=arrived.at[way],
            send_sem=away_send.at[way],
            recv_sem=away_recv.at[way],
            device_id=(dom, (left, right)[way]),
            device_id_type=MESH,
        )

    leave = [leaving(way) for way in range(2)]
    for way in range(2):
        side = 2 * way
        away[way] = (totals[side_ends[side + 1]] - totals[side_ends[side]]).astype(BF16)
        leave[way].start()
    here = totals[side_ends[2]] - totals[side_ends[1]]
    for way in range(2):
        leave[way].wait_recv()
    result = here + arrived[0].astype(F32) + arrived[1].astype(F32)
    for j in range(CSLOTS):
        out[0, 0, j] = result[:, j * tile:(j + 1) * tile]

    for part in range(2):
        for way in range(2):
            by_row[part][way].wait_send()
        for piece in range(3):
            by_col[part][piece].wait_send()
    for way in range(2):
        leave[way].wait_send()


def body(n_dom, n_col, a_tiles, p_tiles, a_cols, slot_map, aggregate):
    rows_x, rows_y, slots, tile, _ = a_tiles.shape
    tiles = rows_x * rows_y
    wide = CSLOTS * tile
    any_space = pl.BlockSpec(memory_space=pl.ANY)
    scalars = pl.BlockSpec(memory_space=pltpu.SMEM)
    return pl.pallas_call(
        functools.partial(kernel, n_dom, n_col),
        out_shape=jax.ShapeDtypeStruct((1, 1, CSLOTS, tile, tile), F32),
        in_specs=[scalars] * 3 + [any_space] * 2,
        out_specs=pl.BlockSpec(memory_space=pltpu.VMEM),
        scratch_shapes=[
            pltpu.VMEM((tiles * slots, tile, tile), BF16),
            pltpu.VMEM((rows_x + 5, rows_y + 4, tile, tile), BF16),
            pltpu.VMEM((tiles, tile, 2 * tile), BF16),
            pltpu.VMEM((PAIRS + 1, tile, tile), F32),
            pltpu.VMEM((tiles + 1, tile, wide), F32),
            pltpu.VMEM((2, tile, wide), BF16),
            pltpu.VMEM((2, tile, wide), BF16),
            pltpu.SMEM((tiles * 2 * PAIRS,), jnp.int32),
            pltpu.SMEM((tiles * 2 * PAIRS,), jnp.int32),
            pltpu.SMEM((tiles * (CSLOTS + 1),), jnp.int32),
            pltpu.SMEM((tiles,), jnp.int32),
            pltpu.SMEM((SIDES + 1,), jnp.int32),
            pltpu.SemaphoreType.DMA((2,)),
            pltpu.SemaphoreType.DMA((4,)),
            pltpu.SemaphoreType.DMA((4,)),
            pltpu.SemaphoreType.DMA((6,)),
            pltpu.SemaphoreType.DMA((6,)),
            pltpu.SemaphoreType.DMA((2,)),
            pltpu.SemaphoreType.DMA((2,)),
        ],
        compiler_params=pltpu.CompilerParams(
            collective_id=0, has_side_effects=True, vmem_limit_bytes=56 * 2**20
        ),
    )(a_cols, slot_map, aggregate, a_tiles.reshape(tiles * slots, tile, tile), p_tiles)


def solution(mesh):
    in_specs = (
        P("dom", "col", None, None, None),
        P("dom", "col", None, None),
        P("dom", "col", None),
        P("dom", "col", None),
        P("dom", "col"),
    )
    out_specs = P("dom", "col", None, None, None)
    call = functools.partial(body, mesh.shape["dom"], mesh.shape["col"])
    return jax.shard_map(call, mesh=mesh, in_specs=in_specs, out_specs=out_specs, check_vma=False)
```

time: 76.5 us -> 37.3 us (0.49)
  the two profiles are of different devices: /device:TPU:219 before, /device:TPU:8 now
where the time goes in v1:
time: 37.3 us; the launch traced here: 37.1 us
  Pallas kernels  35.4 us (95%)
  local copies, waits for them, and re-layouts  1.67 us (4%)
    pallas_call x1, Pallas kernels, body(): pl.pallas_call(functools.partial(kernel, n_dom, n_col), out_shape=jax.Sha...  35.4 us
    unnamed x1, local copies, waits for them, and re-layouts  1.67 us

profile of v1, /device:TPU:8, one launch (start us, length us, event | category | flops | bytes accessed | tf_op | source)
XLA Modules:
  0.0 37.1 jit_solution(14305467297409318715)
XLA Ops:
  0.0 35.4 %shard_map.55 = f32[1,1,4,128,128]{4,3,2,1,0:T(8,128)} custom-call(s32[2,4,12]{2,1,0:T(4,128)} %a_cols.1, s32[2,4,12]{2,1,0:T(4,128)} %slot_map.1, s32[2,4]{1,0:T(2,128)} %aggregate.1, bf16[96,128,128]{2,1,0:T(8,128)(2,1)} %bitcast.1, bf16[2,4,128,128]{3,2,1,0:T(8,128)(2,1)} %p_hbm.1), custom_call_target="tpu_custom_call" | custom-call | tf_op jit(solution)/shard_map/pallas_call | solution.py:224
  35.4 1.7 %copy.7 = f32[1,1,4,128,128]{4,3,2,1,0:T(8,128)} copy(f32[1,1,4,128,128]{4,3,2,1,0:T(8,128)} %shard_map.55) | data formatting | bytes 524288

commit v2 on v1

v2 whole, which is shorter than its diff:
```python
import functools

import jax
import jax.numpy as jnp
from jax import lax
from jax.experimental import pallas as pl
from jax.experimental.pallas import tpu as pltpu
from jax.sharding import PartitionSpec as P

CSLOTS = 4
SIDES = 3
ROWS = 6
GROUPS = ((1, 2, 5, 6), (0, 3, 4, 7))
MESH = pl.DeviceIdType.MESH
F32 = jnp.float32
BF16 = jnp.bfloat16


def dot(left, right):
    return lax.dot_general(left, right, (((1,), (0,)), ((), ())), preferred_element_type=F32)


def split(value):
    high = value.astype(BF16)
    return high, (value - high.astype(F32)).astype(BF16)


def kernel(
    n_dom, n_col, a_cols_hbm, slot_map_hbm, aggregate_hbm, a_hbm, p_hbm, here, arrived,
    a_tiles, near, wide, p_turned, *scratch,
):
    sums, totals = scratch[:8], scratch[8:10]
    (
        a_cols, slot_map, aggregate, away, pick_a, pick_g, ends, order, side_ends,
        own_sem, small_sem, row_send, row_recv, col_send, col_recv, away_send, away_recv,
    ) = scratch[10:]
    rows_x, rows_y, slots = a_cols.shape
    tiles = rows_x * rows_y
    tile = p_hbm.shape[-1]
    dom, col = lax.axis_index("dom"), lax.axis_index("col")
    core = lax.rem(col, 2)
    up, down = lax.rem(dom + 1, n_dom), lax.rem(dom + n_dom - 1, n_dom)
    right, left = lax.rem(col + 1, n_col), lax.rem(col + n_col - 1, n_col)
    outer, inner = jnp.where(core == 0, left, right), jnp.where(core == 0, right, left)
    columns = (3 * core, 1 + core, 3 - 3 * core, 2 - core)
    landing = (5 - 5 * core, 7 - 7 * core, 5 * core, 7 * core)

    own_p = [
        pltpu.make_async_copy(p_hbm.at[:, y], near.at[pl.ds((y + 1) * ROWS + 2, 2)], own_sem.at[y])
        for y in range(rows_y)
    ]
    own_a = pltpu.make_async_copy(a_hbm, a_tiles, own_sem.at[4])
    widen = pltpu.make_async_copy(near, wide.at[pl.ds(ROWS, 6 * ROWS)], own_sem.at[5])
    for copy in own_p:
        copy.start()
    own_a.start()
    small = [
        pltpu.make_async_copy(source, target, small_sem.at[i])
        for i, (source, target) in enumerate(
            ((a_cols_hbm, a_cols), (slot_map_hbm, slot_map), (aggregate_hbm, aggregate))
        )
    ]
    for copy in small:
        copy.start()

    barrier = pltpu.get_barrier_semaphore()
    for target in ((up, col), (down, col), (dom, right), (dom, left)):
        pl.semaphore_signal(barrier, inc=1, device_id=target, device_id_type=MESH)
    pl.semaphore_wait(barrier, 4)

    def along_dom(part, way):
        index = part * 2 + way
        return pltpu.make_async_remote_copy(
            src_ref=p_hbm.at[:, columns[part]],
            dst_ref=near.at[pl.ds((columns[part] + 1) * ROWS + 4 * way, 2)],
            send_sem=row_send.at[index],
            recv_sem=row_recv.at[index],
            device_id=((up, down)[way], col),
            device_id_type=MESH,
        )

    def along_col(part, piece):
        index = part * 3 + piece
        if piece == 1:
            source = p_hbm.at[:, columns[part]]
        else:
            source = near.at[pl.ds((columns[part] + 1) * ROWS + 2 * piece, 2)]
        target = near if part % 2 == 0 else wide
        return pltpu.make_async_remote_copy(
            src_ref=source,
            dst_ref=target.at[pl.ds(landing[part] * ROWS + 2 * piece, 2)],
            send_sem=col_send.at[index],
            recv_sem=col_recv.at[index],
            device_id=(dom, (outer, outer, inner, inner)[part]),
            device_id_type=MESH,
        )

    by_row = [[along_dom(part, way) for way in range(2)] for part in range(4)]
    by_col = [[along_col(part, piece) for piece in range(3)] for part in range(4)]
    for part in range(4):
        by_row[part][0].start()
        by_row[part][1].start()
        by_col[part][1].start()

    for copy in small:
        copy.wait()

    width_y = rows_y * n_col
    origin = (dom * rows_x - 2) * width_y + col * rows_y - 2
    inverse = -(-65536 // width_y)

    def tabulate(t, first_column, most):
        x, y = t // rows_y, t % rows_y
        spots, groups = [], []
        for k in range(slots):
            where = a_cols[x, y, k]
            offset = where - origin
            near_x = (offset * inverse) >> 16
            spot = (offset - near_x * width_y - first_column) * ROWS + near_x
            spots.append(jnp.clip(spot, 0, most))
            groups.append(jnp.where(where >= 0, slot_map[x, y, k], CSLOTS))
        count = jnp.int32(0)
        places = [jnp.int32(-1)] * slots
        ends[t * (CSLOTS + 1)] = 0
        for j in range(CSLOTS):
            for k in range(slots):
                member = groups[k] == j
                places[k] = jnp.where(member, count, places[k])
                count = count + member.astype(jnp.int32)
            ends[t * (CSLOTS + 1) + j + 1] = count
        for place in range(slots):
            slot, spot = jnp.int32(0), jnp.int32(0)
            for k in range(slots):
                chosen = places[k] == place
                slot = jnp.where(chosen, k, slot)
                spot = jnp.where(chosen, spots[k], spot)
            pick_a[t * slots + place] = t * slots + slot
            pick_g[t * slots + place] = spot

    def put_in_order(group):
        members = GROUPS[group]
        sides = [
            lax.rem(aggregate[t // rows_y, t % rows_y], n_col) - col + 1 for t in members
        ]
        count = jnp.int32(0)
        places = [jnp.int32(0)] * len(members)
        side_ends[group * (SIDES + 1)] = 0
        for side in range(SIDES):
            for i in range(len(members)):
                member = sides[i] == side
                places[i] = jnp.where(member, count, places[i])
                count = count + member.astype(jnp.int32)
            side_ends[group * (SIDES + 1) + side + 1] = count
        for place in range(len(members)):
            chosen = jnp.int32(members[0])
            for i, t in enumerate(members):
                chosen = jnp.where(places[i] == place, t, chosen)
            order[group * len(members) + place] = chosen

    def forward(part):
        for way in range(2):
            by_row[part][way].wait_recv()
            by_col[part][2 * way].start()

    for t in GROUPS[0]:
        tabulate(t, 1, 6 * ROWS - 1)
    forward(0)
    for t in GROUPS[1]:
        tabulate(t, 0, 8 * ROWS - 1)
    forward(1)
    put_in_order(0)
    put_in_order(1)
    for copy in own_p:
        copy.wait()
    for t in range(tiles):
        turned = near[(1 + t % rows_y) * ROWS + 2 + t // rows_y].T
        p_turned[t] = jnp.concatenate([turned, turned], axis=1)
    own_a.wait()
    for i in range(8):
        sums[i][0] = jnp.zeros((tile, tile), F32)
    for group in range(2):
        totals[group][0] = jnp.zeros(totals[group].shape[1:], F32)
    forward(2)
    forward(3)
    for part in (0, 2):
        for piece in (1, 0, 2):
            by_col[part][piece].wait_recv()
    widen.start()

    def multiply(group, tiles_g):
        count = len(GROUPS[group])
        ts = [order[group * count + i] for i in range(count)]
        total_refs = totals[group]
        for i in range(count + 1):
            if i < count:
                total = None
                for place in range(slots):
                    at = ts[i] * slots + place
                    term = dot(a_tiles[pick_a[at]], tiles_g[pick_g[at]])
                    total = term if total is None else total + term
                    sums[group * count + i][place + 1] = total
            if i > 0:
                t = ts[i - 1]
                own_sums = sums[group * count + i - 1]
                highs, lows = [], []
                for j in range(CSLOTS):
                    base = t * (CSLOTS + 1) + j
                    high, low = split(own_sums[ends[base + 1]] - own_sums[ends[base]])
                    highs.append(high)
                    lows.append(low)
                stacked = jnp.concatenate(
                    [jnp.concatenate(highs, axis=1), jnp.concatenate(lows, axis=1)], axis=0
                )
                total_refs[i] = total_refs[i - 1] + dot(p_turned[t], stacked)

    multiply(0, near)
    for part in (1, 3):
        for piece in (1, 0, 2):
            by_col[part][piece].wait_recv()
    widen.wait()
    multiply(1, wide)

    def of_side(side):
        value = None
        for group in range(2):
            at = group * (SIDES + 1) + side
            part = totals[group][side_ends[at + 1]] - totals[group][side_ends[at]]
            value = part if value is None else value + part
        return value

    leave = []
    for partner in range(2):
        side = (2 * core, 2 - 2 * core)[partner]
        value = of_side(side).astype(BF16)
        for j in range(CSLOTS):
            away[partner, j] = value[:, j * tile:(j + 1) * tile]
        copy = pltpu.make_async_remote_copy(
            src_ref=away.at[partner],
            dst_ref=arrived.at[partner],
            send_sem=away_send.at[partner],
            recv_sem=away_recv.at[partner],
            device_id=(dom, (outer, inner)[partner]),
            device_id_type=MESH,
        )
        copy.start()
        leave.append(copy)
    value = of_side(1)
    for j in range(CSLOTS):
        here[j] = value[:, j * tile:(j + 1) * tile]

    for part in range(4):
        for way in range(2):
            by_row[part][way].wait_send()
        for piece in range(3):
            by_col[part][piece].wait_send()
    for copy in leave:
        copy.wait()


def body(n_dom, n_col, a_tiles, p_tiles, a_cols, slot_map, aggregate):
    rows_x, rows_y, slots, tile, _ = a_tiles.shape
    tiles = rows_x * rows_y
    across = CSLOTS * tile
    any_space = pl.BlockSpec(memory_space=pl.ANY)
    operands = (a_cols, slot_map, aggregate, a_tiles.reshape(tiles * slots, tile, tile), p_tiles)
    here, arrived = pl.pallas_call(
        functools.partial(kernel, n_dom, n_col),
        out_shape=(
            pltpu.VMEM((CSLOTS, tile, tile), F32),
            pltpu.VMEM((2, CSLOTS, tile, tile), BF16),
        ),
        in_specs=[any_space] * 5,
        out_specs=(pl.BlockSpec(memory_space=pltpu.VMEM), any_space),
        scratch_shapes=[
            pltpu.VMEM((tiles * slots, tile, tile), BF16),
            pltpu.VMEM((6 * ROWS, tile, tile), BF16),
            pltpu.VMEM((8 * ROWS, tile, tile), BF16),
            pltpu.VMEM((tiles, tile, 2 * tile), BF16),
        ]
        + [pltpu.VMEM((slots + 1, tile, tile), F32)] * tiles
        + [pltpu.VMEM((tiles // 2 + 1, tile, across), F32)] * 2
        + [
            pltpu.SMEM(a_cols.shape, jnp.int32),
            pltpu.SMEM(slot_map.shape, jnp.int32),
            pltpu.SMEM(aggregate.shape, jnp.int32),
            pltpu.VMEM((2, CSLOTS, tile, tile), BF16),
            pltpu.SMEM((tiles * slots,), jnp.int32),
            pltpu.SMEM((tiles * slots,), jnp.int32),
            pltpu.SMEM((tiles * (CSLOTS + 1),), jnp.int32),
            pltpu.SMEM((tiles,), jnp.int32),
            pltpu.SMEM((2 * (SIDES + 1),), jnp.int32),
            pltpu.SemaphoreType.DMA((6,)),
            pltpu.SemaphoreType.DMA((3,)),
            pltpu.SemaphoreType.DMA((8,)),
            pltpu.SemaphoreType.DMA((8,)),
            pltpu.SemaphoreType.DMA((12,)),
            pltpu.SemaphoreType.DMA((12,)),
            pltpu.SemaphoreType.DMA((2,)),
            pltpu.SemaphoreType.DMA((2,)),
        ],
        compiler_params=pltpu.CompilerParams(
            collective_id=0, has_side_effects=True, vmem_limit_bytes=24 * 2**20
        ),
    )(*(pltpu.with_memory_space_constraint(operand, pltpu.HBM) for operand in operands))
    result = here + arrived[0].astype(F32) + arrived[1].astype(F32)
    return result[None, None]


def solution(mesh):
    in_specs = (
        P("dom", "col", None, None, None),
        P("dom", "col", None, None),
        P("dom", "col", None),
        P("dom", "col", None),
        P("dom", "col"),
    )
    out_specs = P("dom", "col", None, None, None)
    call = functools.partial(body, mesh.shape["dom"], mesh.shape["col"])
    return jax.shard_map(call, mesh=mesh, in_specs=in_specs, out_specs=out_specs, check_vma=False)
```

time: 37.3 us -> 32.3 us (0.87)
  Pallas kernels: 35.4 us -> 31.5 us
  local copies, waits for them, and re-layouts: 1.67 us -> 0 us
  other arithmetic: 0 us -> 0.74 us
    pallas_call x1, Pallas kernels: 35.4 us -> 31.5 us  [body(): pl.pallas_call(functools.partial(kernel, n_dom, n_col), out_shape=(pltpu....]
    unnamed x1 -> x0, local copies, waits for them, and re-layouts: 1.67 us -> none
    broadcast_in_dim x0 -> x1, other arithmetic: none -> 0.74 us  [body(): return result[None, None]]
where the time goes in v2:
time: 32.3 us; the launch traced here: 32.2 us
  Pallas kernels  31.5 us (98%)
  other arithmetic  0.74 us (2%)
    pallas_call x1, Pallas kernels, body(): pl.pallas_call(functools.partial(kernel, n_dom, n_col), out_shape=(pltpu....  31.5 us
    broadcast_in_dim x1, other arithmetic, body(): return result[None, None]  0.74 us

profile of v2, /device:TPU:8, one launch (start us, length us, event | category | flops | bytes accessed | tf_op | source)
XLA Modules:
  0.0 32.2 jit_solution(11305634812447101824)
XLA Ops:
  0.0 31.5 %shard_map.55 = (f32[4,128,128]{2,1,0:T(8,128)S(1)}, bf16[2,4,128,128]{3,2,1,0:T(8,128)(2,1)S(1)}) custom-call(s32[2,4,12]{2,1,0:T(4,128)} %a_cols_hbm.1, s32[2,4,12]{2,1,0:T(4,128)} %slot_map_hbm.1, s32[2,4]{1,0:T(2,128)} %aggregate_hbm.1, bf16[96,128,128]{2,1,0:T(8,128)(2,1)} %bitcast.9, bf16[2,4,128,128]{3,2,1,0:T(8,128)(2,1)} %p_hbm.1), custom_call_target="tpu_custom_call" | custom-call | tf_op jit(solution)/shard_map/pallas_call | solution.py:266
  31.5 0.7 %fusion = f32[1,1,4,128,128]{4,3,2,1,0:T(8,128)} fusion(f32[4,128,128]{2,1,0:T(8,128)S(1)} %get-tuple-element.7, bf16[2,4,128,128]{3,2,1,0:T(8,128)(2,1)S(1)} %get-tuple-element.8), kind=kLoop, calls=%fused_computation.1 | loop fusion | flops 262144 | bytes 786432 | tf_op jit(solution)/shard_map/broadcast_in_dim | solution.py:306

commit v3 on v2

--- a/solution.py
+++ b/solution.py
@@ -18,6 +18,11 @@
 
 def dot(left, right):
     return lax.dot_general(left, right, (((1,), (0,)), ((), ())), preferred_element_type=F32)
+
+
+def given(*conditions):
+    conditions = [condition for condition in conditions if condition is not None]
+    return pl.when(functools.reduce(jnp.logical_and, conditions)) if conditions else lambda step: step()
 
 
 def split(value):
@@ -39,9 +44,11 @@
     tile = p_hbm.shape[-1]
     dom, col = lax.axis_index("dom"), lax.axis_index("col")
     core = lax.rem(col, 2)
-    up, down = lax.rem(dom + 1, n_dom), lax.rem(dom + n_dom - 1, n_dom)
-    right, left = lax.rem(col + 1, n_col), lax.rem(col + n_col - 1, n_col)
-    outer, inner = jnp.where(core == 0, left, right), jnp.where(core == 0, right, left)
+    outer, inner = col + 2 * core - 1, col + 1 - 2 * core
+    has_up, has_down = dom < n_dom - 1, dom > 0
+    has_outer = (outer >= 0) & (outer < n_col)
+    takes, gives = (has_up, has_down), (has_down, has_up)
+    holds = (has_down, None, has_up)
     columns = (3 * core, 1 + core, 3 - 3 * core, 2 - core)
     landing = (5 - 5 * core, 7 - 7 * core, 5 * core, 7 * core)
 
@@ -64,9 +71,16 @@
         copy.start()
 
     barrier = pltpu.get_barrier_semaphore()
-    for target in ((up, col), (down, col), (dom, right), (dom, left)):
-        pl.semaphore_signal(barrier, inc=1, device_id=target, device_id_type=MESH)
-    pl.semaphore_wait(barrier, 4)
+    for exists, target in (
+        (has_up, (dom + 1, col)), (has_down, (dom - 1, col)), (has_outer, (dom, outer)), (None, (dom, inner))
+    ):
+        given(exists)(
+            functools.partial(
+                pl.semaphore_signal, barrier, inc=1, device_id=target, device_id_type=MESH
+            )
+        )
+    neighbours = 1 + has_up.astype(jnp.int32) + has_down.astype(jnp.int32) + has_outer.astype(jnp.int32)
+    pl.semaphore_wait(barrier, neighbours)
 
     def along_dom(part, way):
         index = part * 2 + way
@@ -75,7 +89,7 @@
             dst_ref=near.at[pl.ds((columns[part] + 1) * ROWS + 4 * way, 2)],
             send_sem=row_send.at[index],
             recv_sem=row_recv.at[index],
-            device_id=((up, down)[way], col),
+            device_id=(dom + 1 - 2 * way, col),
             device_id_type=MESH,
         )
 
@@ -97,10 +111,11 @@
 
     by_row = [[along_dom(part, way) for way in range(2)] for part in range(4)]
     by_col = [[along_col(part, piece) for piece in range(3)] for part in range(4)]
+    partners = (has_outer, has_outer, None, None)
     for part in range(4):
-        by_row[part][0].start()
-        by_row[part][1].start()
-        by_col[part][1].start()
+        for way in range(2):
+            given(takes[way])(by_row[part][way].start)
+        given(partners[part])(by_col[part][1].start)
 
     for copy in small:
         copy.wait()
@@ -129,7 +144,7 @@
                 count = count + member.astype(jnp.int32)
             ends[t * (CSLOTS + 1) + j + 1] = count
         for place in range(slots):
-            slot, spot = jnp.int32(0), jnp.int32(0)
+            slot, spot = jnp.int32(0), jnp.int32((y + 2 - first_column) * ROWS + x + 2)
             for k in range(slots):
                 chosen = places[k] == place
                 slot = jnp.where(chosen, k, slot)
@@ -159,8 +174,10 @@
 
     def forward(part):
         for way in range(2):
-            by_row[part][way].wait_recv()
-            by_col[part][2 * way].start()
+            @given(gives[way])
+            def _():
+                by_row[part][way].wait_recv()
+                given(partners[part])(by_col[part][2 * way].start)
 
     for t in GROUPS[0]:
         tabulate(t, 1, 6 * ROWS - 1)
@@ -184,7 +201,7 @@
     forward(3)
     for part in (0, 2):
         for piece in (1, 0, 2):
-            by_col[part][piece].wait_recv()
+            given(partners[part], holds[piece])(by_col[part][piece].wait_recv)
     widen.start()
 
     def multiply(group, tiles_g):
@@ -216,7 +233,7 @@
     multiply(0, near)
     for part in (1, 3):
         for piece in (1, 0, 2):
-            by_col[part][piece].wait_recv()
+            given(partners[part], holds[piece])(by_col[part][piece].wait_recv)
     widen.wait()
     multiply(1, wide)
 
@@ -229,6 +246,7 @@
         return value
 
     leave = []
+    kept = pltpu.make_async_copy(away.at[0], arrived.at[0], own_sem.at[6])
     for partner in range(2):
         side = (2 * core, 2 - 2 * core)[partner]
         value = of_side(side).astype(BF16)
@@ -242,19 +260,21 @@
             device_id=(dom, (outer, inner)[partner]),
             device_id_type=MESH,
         )
-        copy.start()
+        given((has_outer, None)[partner])(copy.start)
         leave.append(copy)
+    given(jnp.logical_not(has_outer))(kept.start)
     value = of_side(1)
     for j in range(CSLOTS):
         here[j] = value[:, j * tile:(j + 1) * tile]
 
     for part in range(4):
         for way in range(2):
-            by_row[part][way].wait_send()
+            given(takes[way])(by_row[part][way].wait_send)
         for piece in range(3):
-            by_col[part][piece].wait_send()
-    for copy in leave:
-        copy.wait()
+            given(partners[part], holds[piece])(by_col[part][piece].wait_send)
+    leave[1].wait()
+    given(has_outer)(leave[0].wait)
+    given(jnp.logical_not(has_outer))(kept.wait)
 
 
 def body(n_dom, n_col, a_tiles, p_tiles, a_cols, slot_map, aggregate):
@@ -289,7 +309,7 @@
             pltpu.SMEM((tiles * (CSLOTS + 1),), jnp.int32),
             pltpu.SMEM((tiles,), jnp.int32),
             pltpu.SMEM((2 * (SIDES + 1),), jnp.int32),
-            pltpu.SemaphoreType.DMA((6,)),
+            pltpu.SemaphoreType.DMA((7,)),
             pltpu.SemaphoreType.DMA((3,)),
             pltpu.SemaphoreType.DMA((8,)),
             pltpu.SemaphoreType.DMA((8,)),

time: 32.3 us -> 24.1 us (0.75)
  the two profiles are of different devices: /device:TPU:8 before, /device:TPU:9 now
where the time goes in v3:
time: 24.1 us; the launch traced here: 24 us
  Pallas kernels  23.3 us (97%)
  other arithmetic  0.74 us (3%)
    pallas_call x1, Pallas kernels, body(): pl.pallas_call(functools.partial(kernel, n_dom, n_col), out_shape=(pltpu....  23.3 us
    broadcast_in_dim x1, other arithmetic, body(): return result[None, None]  0.74 us

profile of v3, /device:TPU:9, one launch (start us, length us, event | category | flops | bytes accessed | tf_op | source)
XLA Modules:
  0.0 24.0 jit_solution(14768845156102396387)
XLA Ops:
  0.0 23.3 %shard_map.55 = (f32[4,128,128]{2,1,0:T(8,128)S(1)}, bf16[2,4,128,128]{3,2,1,0:T(8,128)(2,1)S(1)}) custom-call(s32[2,4,12]{2,1,0:T(4,128)} %a_cols_hbm.1, s32[2,4,12]{2,1,0:T(4,128)} %slot_map_hbm.1, s32[2,4]{1,0:T(2,128)} %aggregate_hbm.1, bf16[96,128,128]{2,1,0:T(8,128)(2,1)} %bitcast.9, bf16[2,4,128,128]{3,2,1,0:T(8,128)(2,1)} %p_hbm.1), custom_call_target="tpu_custom_call" | custom-call | tf_op jit(solution)/shard_map/pallas_call | solution.py:286
  23.3 0.7 %fusion = f32[1,1,4,128,128]{4,3,2,1,0:T(8,128)} fusion(f32[4,128,128]{2,1,0:T(8,128)S(1)} %get-tuple-element.7, bf16[2,4,128,128]{3,2,1,0:T(8,128)(2,1)S(1)} %get-tuple-element.8), kind=kLoop, calls=%fused_computation.1 | loop fusion | flops 262144 | bytes 786432 | tf_op jit(solution)/shard_map/broadcast_in_dim | solution.py:326

commit v4 on v3

--- a/solution.py
+++ b/solution.py
@@ -10,7 +10,8 @@
 CSLOTS = 4
 SIDES = 3
 ROWS = 6
-GROUPS = ((1, 2, 5, 6), (0, 3, 4, 7))
+NEAR = 6 * ROWS
+GROUPS = (4, 2, 2)
 MESH = pl.DeviceIdType.MESH
 F32 = jnp.float32
 BF16 = jnp.bfloat16
@@ -32,13 +33,13 @@
 
 def kernel(
     n_dom, n_col, a_cols_hbm, slot_map_hbm, aggregate_hbm, a_hbm, p_hbm, here, arrived,
-    a_tiles, near, wide, p_turned, *scratch,
+    a_tiles, near, far_outer, far_inner, p_turned, *scratch,
 ):
-    sums, totals = scratch[:8], scratch[8:10]
+    sums, totals = scratch[:8], scratch[8:11]
     (
         a_cols, slot_map, aggregate, away, pick_a, pick_g, ends, order, side_ends,
-        own_sem, small_sem, row_send, row_recv, col_send, col_recv, away_send, away_recv,
-    ) = scratch[10:]
+        ready, own_sem, small_sem, row_send, row_recv, col_send, col_recv, away_send, away_recv,
+    ) = scratch[11:]
     rows_x, rows_y, slots = a_cols.shape
     tiles = rows_x * rows_y
     tile = p_hbm.shape[-1]
@@ -50,14 +51,28 @@
     takes, gives = (has_up, has_down), (has_down, has_up)
     holds = (has_down, None, has_up)
     columns = (3 * core, 1 + core, 3 - 3 * core, 2 - core)
-    landing = (5 - 5 * core, 7 - 7 * core, 5 * core, 7 * core)
-
+    landing = (5 - 5 * core, 0, 5 * core, 0)
+    members = ((1, 2, 5, 6), (3 * core, 3 * core + 4), (3 - 3 * core, 7 - 3 * core))
+
+    barrier = pltpu.get_barrier_semaphore()
+    is_first, is_second = core == 0, core == 1
+
+    def tell(semaphore, target, *conditions):
+        given(*conditions)(
+            functools.partial(
+                pl.semaphore_signal, semaphore, inc=1, device_id=target, device_id_type=MESH
+            )
+        )
+
+    tell(barrier, (dom + 1, col), has_up, dom > 0)
+    tell(barrier, (dom - 1, col), has_down)
+    tell(barrier, (dom, inner), col > 0)
+    tell(barrier, (dom, outer), has_outer, is_second)
     own_p = [
         pltpu.make_async_copy(p_hbm.at[:, y], near.at[pl.ds((y + 1) * ROWS + 2, 2)], own_sem.at[y])
         for y in range(rows_y)
     ]
     own_a = pltpu.make_async_copy(a_hbm, a_tiles, own_sem.at[4])
-    widen = pltpu.make_async_copy(near, wide.at[pl.ds(ROWS, 6 * ROWS)], own_sem.at[5])
     for copy in own_p:
         copy.start()
     own_a.start()
@@ -70,17 +85,11 @@
     for copy in small:
         copy.start()
 
-    barrier = pltpu.get_barrier_semaphore()
-    for exists, target in (
-        (has_up, (dom + 1, col)), (has_down, (dom - 1, col)), (has_outer, (dom, outer)), (None, (dom, inner))
-    ):
-        given(exists)(
-            functools.partial(
-                pl.semaphore_signal, barrier, inc=1, device_id=target, device_id_type=MESH
-            )
-        )
-    neighbours = 1 + has_up.astype(jnp.int32) + has_down.astype(jnp.int32) + has_outer.astype(jnp.int32)
-    pl.semaphore_wait(barrier, neighbours)
+    heard = (dom > 1, has_up, col != 1, has_outer & is_first)
+    pl.semaphore_wait(barrier, sum(condition.astype(jnp.int32) for condition in heard))
+    tell(ready.at[0], (dom + 1, col), dom == 0)
+    tell(ready.at[1], (dom, inner), col == 0)
+    tell(ready.at[2], (dom, outer), has_outer, is_first)
 
     def along_dom(part, way):
         index = part * 2 + way
@@ -99,7 +108,7 @@
             source = p_hbm.at[:, columns[part]]
         else:
             source = near.at[pl.ds((columns[part] + 1) * ROWS + 2 * piece, 2)]
-        target = near if part % 2 == 0 else wide
+        target = (near, far_outer, near, far_inner)[part]
         return pltpu.make_async_remote_copy(
             src_ref=source,
             dst_ref=target.at[pl.ds(landing[part] * ROWS + 2 * piece, 2)],
@@ -112,10 +121,18 @@
     by_row = [[along_dom(part, way) for way in range(2)] for part in range(4)]
     by_col = [[along_col(part, piece) for piece in range(3)] for part in range(4)]
     partners = (has_outer, has_outer, None, None)
+    at_once = ((has_outer & is_first,) * 2) + ((col != 1,) * 2)
     for part in range(4):
-        for way in range(2):
-            given(takes[way])(by_row[part][way].start)
-        given(partners[part])(by_col[part][1].start)
+        given(has_up)(by_row[part][0].start)
+        given(dom > 1)(by_row[part][1].start)
+        given(at_once[part])(by_col[part][1].start)
+
+    @pl.when(dom == 1)
+    def _():
+        pl.semaphore_wait(ready.at[0], 1)
+        for part in range(4):
+            by_row[part][1].start()
+
 
     for copy in small:
         copy.wait()
@@ -124,15 +141,16 @@
     origin = (dom * rows_x - 2) * width_y + col * rows_y - 2
     inverse = -(-65536 // width_y)
 
-    def tabulate(t, first_column, most):
-        x, y = t // rows_y, t % rows_y
+    def tabulate(t):
+        x, y = t // rows_y, lax.rem(t, rows_y)
         spots, groups = [], []
         for k in range(slots):
             where = a_cols[x, y, k]
             offset = where - origin
             near_x = (offset * inverse) >> 16
-            spot = (offset - near_x * width_y - first_column) * ROWS + near_x
-            spots.append(jnp.clip(spot, 0, most))
+            near_y = offset - near_x * width_y
+            spot = jnp.where((near_y == 0) | (near_y == 7), NEAR + near_x, (near_y - 1) * ROWS + near_x)
+            spots.append(jnp.clip(spot, 0, NEAR + ROWS - 1))
             groups.append(jnp.where(where >= 0, slot_map[x, y, k], CSLOTS))
         count = jnp.int32(0)
         places = [jnp.int32(-1)] * slots
@@ -144,7 +162,7 @@
                 count = count + member.astype(jnp.int32)
             ends[t * (CSLOTS + 1) + j + 1] = count
         for place in range(slots):
-            slot, spot = jnp.int32(0), jnp.int32((y + 2 - first_column) * ROWS + x + 2)
+            slot, spot = jnp.int32(0), jnp.int32((y + 1) * ROWS + x + 2)
             for k in range(slots):
                 chosen = places[k] == place
                 slot = jnp.where(chosen, k, slot)
@@ -153,24 +171,22 @@
             pick_g[t * slots + place] = spot
 
     def put_in_order(group):
-        members = GROUPS[group]
-        sides = [
-            lax.rem(aggregate[t // rows_y, t % rows_y], n_col) - col + 1 for t in members
-        ]
+        ts, first = members[group], sum(GROUPS[:group])
+        sides = [lax.rem(aggregate[t // rows_y, lax.rem(t, rows_y)], n_col) - col + 1 for t in ts]
         count = jnp.int32(0)
-        places = [jnp.int32(0)] * len(members)
+        places = [jnp.int32(0)] * len(ts)
         side_ends[group * (SIDES + 1)] = 0
         for side in range(SIDES):
-            for i in range(len(members)):
+            for i in range(len(ts)):
                 member = sides[i] == side
                 places[i] = jnp.where(member, count, places[i])
                 count = count + member.astype(jnp.int32)
             side_ends[group * (SIDES + 1) + side + 1] = count
-        for place in range(len(members)):
-            chosen = jnp.int32(members[0])
-            for i, t in enumerate(members):
+        for place in range(len(ts)):
+            chosen = jnp.int32(ts[0])
+            for i, t in enumerate(ts):
                 chosen = jnp.where(places[i] == place, t, chosen)
-            order[group * len(members) + place] = chosen
+            order[first + place] = chosen
 
     def forward(part):
         for way in range(2):
@@ -179,14 +195,21 @@
                 by_row[part][way].wait_recv()
                 given(partners[part])(by_col[part][2 * way].start)
 
-    for t in GROUPS[0]:
-        tabulate(t, 1, 6 * ROWS - 1)
+    for t in members[0]:
+        tabulate(t)
+
+    @pl.when(has_outer & is_second)
+    def _():
+        pl.semaphore_wait(ready.at[2], 1)
+        for part in range(2):
+            by_col[part][1].start()
+
     forward(0)
-    for t in GROUPS[1]:
-        tabulate(t, 0, 8 * ROWS - 1)
+    for t in members[1] + members[2]:
+        tabulate(t)
     forward(1)
-    put_in_order(0)
-    put_in_order(1)
+    for group in range(3):
+        put_in_order(group)
     for copy in own_p:
         copy.wait()
     for t in range(tiles):
@@ -195,58 +218,75 @@
     own_a.wait()
     for i in range(8):
         sums[i][0] = jnp.zeros((tile, tile), F32)
-    for group in range(2):
+    for group in range(3):
         totals[group][0] = jnp.zeros(totals[group].shape[1:], F32)
+
+    @pl.when(col == 1)
+    def _():
+        pl.semaphore_wait(ready.at[1], 1)
+        for part in (2, 3):
+            by_col[part][1].start()
+
     forward(2)
     forward(3)
     for part in (0, 2):
         for piece in (1, 0, 2):
             given(partners[part], holds[piece])(by_col[part][piece].wait_recv)
-    widen.start()
-
-    def multiply(group, tiles_g):
-        count = len(GROUPS[group])
-        ts = [order[group * count + i] for i in range(count)]
-        total_refs = totals[group]
-        for i in range(count + 1):
-            if i < count:
-                total = None
-                for place in range(slots):
-                    at = ts[i] * slots + place
-                    term = dot(a_tiles[pick_a[at]], tiles_g[pick_g[at]])
-                    total = term if total is None else total + term
-                    sums[group * count + i][place + 1] = total
-            if i > 0:
-                t = ts[i - 1]
-                own_sums = sums[group * count + i - 1]
-                highs, lows = [], []
-                for j in range(CSLOTS):
-                    base = t * (CSLOTS + 1) + j
-                    high, low = split(own_sums[ends[base + 1]] - own_sums[ends[base]])
-                    highs.append(high)
-                    lows.append(low)
-                stacked = jnp.concatenate(
-                    [jnp.concatenate(highs, axis=1), jnp.concatenate(lows, axis=1)], axis=0
+
+    ts = [order[i] for i in range(tiles)]
+
+    def slot_sums(i, far):
+        total = None
+        for place in range(slots):
+            at = ts[i] * slots + place
+            spot = pick_g[at]
+            if far is None:
+                right = near[jnp.minimum(spot, NEAR - 1)]
+            else:
+                right = jnp.where(
+                    spot >= NEAR, far[jnp.maximum(spot - NEAR, 0)], near[jnp.minimum(spot, NEAR - 1)]
                 )
-                total_refs[i] = total_refs[i - 1] + dot(p_turned[t], stacked)
-
-    multiply(0, near)
-    for part in (1, 3):
-        for piece in (1, 0, 2):
-            given(partners[part], holds[piece])(by_col[part][piece].wait_recv)
-    widen.wait()
-    multiply(1, wide)
+            term = dot(a_tiles[pick_a[at]], right)
+            total = term if total is None else total + term
+            sums[i][place + 1] = total
+
+    def coarse_sums(i, group):
+        place = i - sum(GROUPS[:group])
+        t = ts[i]
+        highs, lows = [], []
+        for j in range(CSLOTS):
+            base = t * (CSLOTS + 1) + j
+            high, low = split(sums[i][ends[base + 1]] - sums[i][ends[base]])
+            highs.append(high)
+            lows.append(low)
+        stacked = jnp.concatenate(
+            [jnp.concatenate(highs, axis=1), jnp.concatenate(lows, axis=1)], axis=0
+        )
+        totals[group][place + 1] = totals[group][place] + dot(p_turned[t], stacked)
+
+    group_of = [group for group, size in enumerate(GROUPS) for _ in range(size)]
+    for i in range(tiles + 1):
+        if i == GROUPS[0]:
+            for piece in (1, 0, 2):
+                given(has_outer, holds[piece])(by_col[1][piece].wait_recv)
+        if i == GROUPS[0] + GROUPS[1]:
+            for piece in (1, 0, 2):
+                given(holds[piece])(by_col[3][piece].wait_recv)
+        if i < tiles:
+            slot_sums(i, (None, far_outer, far_inner)[group_of[i]])
+        if i > 0:
+            coarse_sums(i - 1, group_of[i - 1])
 
     def of_side(side):
         value = None
-        for group in range(2):
+        for group in range(3):
             at = group * (SIDES + 1) + side
             part = totals[group][side_ends[at + 1]] - totals[group][side_ends[at]]
             value = part if value is None else value + part
         return value
 
     leave = []
-    kept = pltpu.make_async_copy(away.at[0], arrived.at[0], own_sem.at[6])
+    kept = pltpu.make_async_copy(away.at[0], arrived.at[0], own_sem.at[5])
     for partner in range(2):
         side = (2 * core, 2 - 2 * core)[partner]
         value = of_side(side).astype(BF16)
@@ -293,12 +333,13 @@
         out_specs=(pl.BlockSpec(memory_space=pltpu.VMEM), any_space),
         scratch_shapes=[
             pltpu.VMEM((tiles * slots, tile, tile), BF16),
-            pltpu.VMEM((6 * ROWS, tile, tile), BF16),
-            pltpu.VMEM((8 * ROWS, tile, tile), BF16),
+            pltpu.VMEM((NEAR, tile, tile), BF16),
+            pltpu.VMEM((ROWS, tile, tile), BF16),
+            pltpu.VMEM((ROWS, tile, tile), BF16),
             pltpu.VMEM((tiles, tile, 2 * tile), BF16),
         ]
         + [pltpu.VMEM((slots + 1, tile, tile), F32)] * tiles
-        + [pltpu.VMEM((tiles // 2 + 1, tile, across), F32)] * 2
+        + [pltpu.VMEM((size + 1, tile, across), F32) for size in GROUPS]
         + [
             pltpu.SMEM(a_cols.shape, jnp.int32),
             pltpu.SMEM(slot_map.shape, jnp.int32),
@@ -308,8 +349,9 @@
             pltpu.SMEM((tiles * slots,), jnp.int32),
             pltpu.SMEM((tiles * (CSLOTS + 1),), jnp.int32),
             pltpu.SMEM((tiles,), jnp.int32),
-            pltpu.SMEM((2 * (SIDES + 1),), jnp.int32),
-            pltpu.SemaphoreType.DMA((7,)),
+            pltpu.SMEM((3 * (SIDES + 1),), jnp.int32),
+            pltpu.SemaphoreType.REGULAR((3,)),
+            pltpu.SemaphoreType.DMA((6,)),
             pltpu.SemaphoreType.DMA((3,)),
             pltpu.SemaphoreType.DMA((8,)),
             pltpu.SemaphoreType.DMA((8,)),

time: 24.1 us -> 23.4 us (0.971)
  the two profiles are of different devices: /device:TPU:9 before, /device:TPU:1 now
where the time goes in v4:
time: 23.4 us; the launch traced here: 23.3 us
  Pallas kernels  22.5 us (96%)
  other arithmetic  0.74 us (3%)
    pallas_call x1, Pallas kernels, body(): pl.pallas_call(functools.partial(kernel, n_dom, n_col), out_shape=(pltpu....  22.5 us
    broadcast_in_dim x1, other arithmetic, body(): return result[None, None]  0.74 us

profile of v4, /device:TPU:1, one launch (start us, length us, event | category | flops | bytes accessed | tf_op | source)
XLA Modules:
  0.0 23.3 jit_solution(955090396888672399)
XLA Ops:
  0.0 22.5 %shard_map.55 = (f32[4,128,128]{2,1,0:T(8,128)S(1)}, bf16[2,4,128,128]{3,2,1,0:T(8,128)(2,1)S(1)}) custom-call(s32[2,4,12]{2,1,0:T(4,128)} %a_cols_hbm.1, s32[2,4,12]{2,1,0:T(4,128)} %slot_map_hbm.1, s32[2,4]{1,0:T(2,128)} %aggregate_hbm.1, bf16[96,128,128]{2,1,0:T(8,128)(2,1)} %bitcast.9, bf16[2,4,128,128]{3,2,1,0:T(8,128)(2,1)} %p_hbm.1), custom_call_target="tpu_custom_call" | custom-call | tf_op jit(solution)/shard_map/pallas_call | solution.py:326
  22.6 0.7 %fusion = f32[1,1,4,128,128]{4,3,2,1,0:T(8,128)} fusion(f32[4,128,128]{2,1,0:T(8,128)S(1)} %get-tuple-element.7, bf16[2,4,128,128]{3,2,1,0:T(8,128)(2,1)S(1)} %get-tuple-element.8), kind=kLoop, calls=%fused_computation.1 | loop fusion | flops 262144 | bytes 786432 | tf_op jit(solution)/shard_map/broadcast_in_dim | solution.py:368

commit v5 on v4

--- a/solution.py
+++ b/solution.py
@@ -49,7 +49,6 @@
     has_up, has_down = dom < n_dom - 1, dom > 0
     has_outer = (outer >= 0) & (outer < n_col)
     takes, gives = (has_up, has_down), (has_down, has_up)
-    holds = (has_down, None, has_up)
     columns = (3 * core, 1 + core, 3 - 3 * core, 2 - core)
     landing = (5 - 5 * core, 0, 5 * core, 0)
     members = ((1, 2, 5, 6), (3 * core, 3 * core + 4), (3 - 3 * core, 7 - 3 * core))
@@ -69,10 +68,10 @@
     tell(barrier, (dom, inner), col > 0)
     tell(barrier, (dom, outer), has_outer, is_second)
     own_p = [
-        pltpu.make_async_copy(p_hbm.at[:, y], near.at[pl.ds((y + 1) * ROWS + 2, 2)], own_sem.at[y])
+        pltpu.make_async_copy(p_hbm.at[:, y], near.at[pl.ds((y + 1) * ROWS + 2, 2)], own_sem.at[0])
         for y in range(rows_y)
     ]
-    own_a = pltpu.make_async_copy(a_hbm, a_tiles, own_sem.at[4])
+    own_a = pltpu.make_async_copy(a_hbm, a_tiles, own_sem.at[1])
     for copy in own_p:
         copy.start()
     own_a.start()
@@ -91,19 +90,26 @@
     tell(ready.at[1], (dom, inner), col == 0)
     tell(ready.at[2], (dom, outer), has_outer, is_first)
 
+    def arrive(semaphore, count):
+        some = near.at[pl.ds(0, count)]
+        pltpu.make_async_copy(some, some, semaphore).wait()
+
+    def arrive_pieces(semaphore, count, *conditions):
+        given(has_up & has_down, *conditions)(lambda: arrive(semaphore, 3 * count))
+        given(has_up ^ has_down, *conditions)(lambda: arrive(semaphore, 2 * count))
+
     def along_dom(part, way):
         index = part * 2 + way
         return pltpu.make_async_remote_copy(
             src_ref=p_hbm.at[:, columns[part]],
             dst_ref=near.at[pl.ds((columns[part] + 1) * ROWS + 4 * way, 2)],
-            send_sem=row_send.at[index],
+            send_sem=row_send.at[way],
             recv_sem=row_recv.at[index],
             device_id=(dom + 1 - 2 * way, col),
             device_id_type=MESH,
         )
 
     def along_col(part, piece):
-        index = part * 3 + piece
         if piece == 1:
             source = p_hbm.at[:, columns[part]]
         else:
@@ -112,8 +118,8 @@
         return pltpu.make_async_remote_copy(
             src_ref=source,
             dst_ref=target.at[pl.ds(landing[part] * ROWS + 2 * piece, 2)],
-            send_sem=col_send.at[index],
-            recv_sem=col_recv.at[index],
+            send_sem=col_send.at[part // 2],
+            recv_sem=col_recv.at[part],
             device_id=(dom, (outer, outer, inner, inner)[part]),
             device_id_type=MESH,
         )
@@ -210,8 +216,7 @@
     forward(1)
     for group in range(3):
         put_in_order(group)
-    for copy in own_p:
-        copy.wait()
+    arrive(own_sem.at[0], tiles)
     for t in range(tiles):
         turned = near[(1 + t % rows_y) * ROWS + 2 + t // rows_y].T
         p_turned[t] = jnp.concatenate([turned, turned], axis=1)
@@ -230,8 +235,7 @@
     forward(2)
     forward(3)
     for part in (0, 2):
-        for piece in (1, 0, 2):
-            given(partners[part], holds[piece])(by_col[part][piece].wait_recv)
+        arrive_pieces(col_recv.at[part], 2, partners[part])
 
     ts = [order[i] for i in range(tiles)]
 
@@ -267,11 +271,9 @@
     group_of = [group for group, size in enumerate(GROUPS) for _ in range(size)]
     for i in range(tiles + 1):
         if i == GROUPS[0]:
-            for piece in (1, 0, 2):
-                given(has_outer, holds[piece])(by_col[1][piece].wait_recv)
+            arrive_pieces(col_recv.at[1], 2, has_outer)
         if i == GROUPS[0] + GROUPS[1]:
-            for piece in (1, 0, 2):
-                given(holds[piece])(by_col[3][piece].wait_recv)
+            arrive_pieces(col_recv.at[3], 2)
         if i < tiles:
             slot_sums(i, (None, far_outer, far_inner)[group_of[i]])
         if i > 0:
@@ -286,7 +288,7 @@
         return value
 
     leave = []
-    kept = pltpu.make_async_copy(away.at[0], arrived.at[0], own_sem.at[5])
+    kept = pltpu.make_async_copy(away.at[0], arrived.at[0], own_sem.at[2])
     for partner in range(2):
         side = (2 * core, 2 - 2 * core)[partner]
         value = of_side(side).astype(BF16)
@@ -307,11 +309,10 @@
     for j in range(CSLOTS):
         here[j] = value[:, j * tile:(j + 1) * tile]
 
-    for part in range(4):
-        for way in range(2):
-            given(takes[way])(by_row[part][way].wait_send)
-        for piece in range(3):
-            given(partners[part], holds[piece])(by_col[part][piece].wait_send)
+    for way in range(2):
+        given(takes[way])(functools.partial(arrive, row_send.at[way], tiles))
+    arrive_pieces(col_send.at[0], 4, has_outer)
+    arrive_pieces(col_send.at[1], 4)
     leave[1].wait()
     given(has_outer)(leave[0].wait)
     given(jnp.logical_not(has_outer))(kept.wait)
@@ -351,12 +352,12 @@
             pltpu.SMEM((tiles,), jnp.int32),
             pltpu.SMEM((3 * (SIDES + 1),), jnp.int32),
             pltpu.SemaphoreType.REGULAR((3,)),
-            pltpu.SemaphoreType.DMA((6,)),
             pltpu.SemaphoreType.DMA((3,)),
+            pltpu.SemaphoreType.DMA((3,)),
+            pltpu.SemaphoreType.DMA((2,)),
             pltpu.SemaphoreType.DMA((8,)),
-            pltpu.SemaphoreType.DMA((8,)),
-            pltpu.SemaphoreType.DMA((12,)),
-            pltpu.SemaphoreType.DMA((12,)),
+            pltpu.SemaphoreType.DMA((2,)),
+            pltpu.SemaphoreType.DMA((4,)),
             pltpu.SemaphoreType.DMA((2,)),
             pltpu.SemaphoreType.DMA((2,)),
         ],

time: 23.4 us -> 23.2 us (level)
    pallas_call x1, Pallas kernels: 22.5 us -> 22.3 us  [body(): pl.pallas_call(functools.partial(kernel, n_dom, n_col), out_shape=(pltpu....]
where the time goes in v5:
time: 23.2 us; the launch traced here: 23.1 us
  Pallas kernels  22.3 us (96%)
  other arithmetic  0.74 us (3%)
    pallas_call x1, Pallas kernels, body(): pl.pallas_call(functools.partial(kernel, n_dom, n_col), out_shape=(pltpu....  22.3 us
    broadcast_in_dim x1, other arithmetic, body(): return result[None, None]  0.74 us

profile of v5, /device:TPU:1, one launch (start us, length us, event | category | flops | bytes accessed | tf_op | source)
XLA Modules:
  0.0 23.1 jit_solution(2336213570889814514)
XLA Ops:
  0.0 22.3 %shard_map.55 = (f32[4,128,128]{2,1,0:T(8,128)S(1)}, bf16[2,4,128,128]{3,2,1,0:T(8,128)(2,1)S(1)}) custom-call(s32[2,4,12]{2,1,0:T(4,128)} %a_cols_hbm.1, s32[2,4,12]{2,1,0:T(4,128)} %slot_map_hbm.1, s32[2,4]{1,0:T(2,128)} %aggregate_hbm.1, bf16[96,128,128]{2,1,0:T(8,128)(2,1)} %bitcast.9, bf16[2,4,128,128]{3,2,1,0:T(8,128)(2,1)} %p_hbm.1), custom_call_target="tpu_custom_call" | custom-call | tf_op jit(solution)/shard_map/pallas_call | solution.py:327
  22.3 0.7 %fusion = f32[1,1,4,128,128]{4,3,2,1,0:T(8,128)} fusion(f32[4,128,128]{2,1,0:T(8,128)S(1)} %get-tuple-element.7, bf16[2,4,128,128]{3,2,1,0:T(8,128)(2,1)S(1)} %get-tuple-element.8), kind=kLoop, calls=%fused_computation.1 | loop fusion | flops 262144 | bytes 786432 | tf_op jit(solution)/shard_map/broadcast_in_dim | solution.py:369

commit v6 on v5

--- a/solution.py
+++ b/solution.py
@@ -33,12 +33,12 @@
 
 def kernel(
     n_dom, n_col, a_cols_hbm, slot_map_hbm, aggregate_hbm, a_hbm, p_hbm, here, arrived,
-    a_tiles, near, far_outer, far_inner, p_turned, *scratch,
+    a_tiles, near, far_outer, far_inner, relayed, p_turned, *scratch,
 ):
     sums, totals = scratch[:8], scratch[8:11]
     (
         a_cols, slot_map, aggregate, away, pick_a, pick_g, ends, order, side_ends,
-        ready, own_sem, small_sem, row_send, row_recv, col_send, col_recv, away_send, away_recv,
+        ready, relay_send, relay_recv, own_sem, small_sem, row_send, row_recv, col_send, col_recv, away_send, away_recv,
     ) = scratch[11:]
     rows_x, rows_y, slots = a_cols.shape
     tiles = rows_x * rows_y
@@ -63,7 +63,9 @@
             )
         )
 
+    is_relay, is_source = (dom == 0) & (col == 1), (dom == 1) & (col == 0)
     tell(barrier, (dom + 1, col), has_up, dom > 0)
+    tell(barrier, (dom + 1, inner), is_relay)
     tell(barrier, (dom - 1, col), has_down)
     tell(barrier, (dom, inner), col > 0)
     tell(barrier, (dom, outer), has_outer, is_second)
@@ -84,9 +86,9 @@
     for copy in small:
         copy.start()
 
-    heard = (dom > 1, has_up, col != 1, has_outer & is_first)
+    heard = (dom > 1, has_up, col != 1, has_outer & is_first, is_source)
     pl.semaphore_wait(barrier, sum(condition.astype(jnp.int32) for condition in heard))
-    tell(ready.at[0], (dom + 1, col), dom == 0)
+    tell(ready.at[0], (dom + 1, col), dom == 0, col > 0)
     tell(ready.at[1], (dom, inner), col == 0)
     tell(ready.at[2], (dom, outer), has_outer, is_first)
 
@@ -124,6 +126,27 @@
             device_id_type=MESH,
         )
 
+    def to_relay(part):
+        return pltpu.make_async_remote_copy(
+            src_ref=p_hbm.at[:, columns[part]],
+            dst_ref=relayed.at[pl.ds(2 * part, 2)],
+            send_sem=row_send.at[1],
+            recv_sem=relay_recv,
+            device_id=(dom - 1, inner),
+            device_id_type=MESH,
+        )
+
+    def hand_on(part):
+        theirs = (0, 1, 3, 2)[part]
+        return pltpu.make_async_remote_copy(
+            src_ref=relayed.at[pl.ds(2 * part, 2)],
+            dst_ref=near.at[pl.ds((theirs + 1) * ROWS + 4, 2)],
+            send_sem=relay_send,
+            recv_sem=row_recv.at[2 * part + 1],
+            device_id=(dom, inner),
+            device_id_type=MESH,
+        )
+
     by_row = [[along_dom(part, way) for way in range(2)] for part in range(4)]
     by_col = [[along_col(part, piece) for piece in range(3)] for part in range(4)]
     partners = (has_outer, has_outer, None, None)
@@ -133,11 +156,16 @@
         given(dom > 1)(by_row[part][1].start)
         given(at_once[part])(by_col[part][1].start)
 
-    @pl.when(dom == 1)
+    @pl.when((dom == 1) & (col > 0))
     def _():
         pl.semaphore_wait(ready.at[0], 1)
         for part in range(4):
             by_row[part][1].start()
+
+    @pl.when(is_source)
+    def _():
+        for part in range(4):
+            to_relay(part).start()
 
 
     for copy in small:
@@ -232,6 +260,12 @@
         for part in (2, 3):
             by_col[part][1].start()
 
+    @pl.when(is_relay)
+    def _():
+        arrive(relay_recv, tiles)
+        for part in range(4):
+            hand_on(part).start()
+
     forward(2)
     forward(3)
     for part in (0, 2):
@@ -311,6 +345,7 @@
 
     for way in range(2):
         given(takes[way])(functools.partial(arrive, row_send.at[way], tiles))
+    given(is_relay)(functools.partial(arrive, relay_send, tiles))
     arrive_pieces(col_send.at[0], 4, has_outer)
     arrive_pieces(col_send.at[1], 4)
     leave[1].wait()
@@ -337,6 +372,7 @@
             pltpu.VMEM((NEAR, tile, tile), BF16),
             pltpu.VMEM((ROWS, tile, tile), BF16),
             pltpu.VMEM((ROWS, tile, tile), BF16),
+            pltpu.VMEM((tiles, tile, tile), BF16),
             pltpu.VMEM((tiles, tile, 2 * tile), BF16),
         ]
         + [pltpu.VMEM((slots + 1, tile, tile), F32)] * tiles
@@ -352,6 +388,8 @@
             pltpu.SMEM((tiles,), jnp.int32),
             pltpu.SMEM((3 * (SIDES + 1),), jnp.int32),
             pltpu.SemaphoreType.REGULAR((3,)),
+            pltpu.SemaphoreType.DMA,
+            pltpu.SemaphoreType.DMA,
             pltpu.SemaphoreType.DMA((3,)),
             pltpu.SemaphoreType.DMA((3,)),
             pltpu.SemaphoreType.DMA((2,)),

time: 23.2 us -> 22.1 us (0.953)
  the two profiles are of different devices: /device:TPU:1 before, /device:TPU:199 now
where the time goes in v6:
time: 22.1 us; the launch traced here: 22 us
  Pallas kernels  21.2 us (96%)
  other arithmetic  0.74 us (3%)
    pallas_call x1, Pallas kernels, body(): pl.pallas_call(functools.partial(kernel, n_dom, n_col), out_shape=(pltpu....  21.2 us
    broadcast_in_dim x1, other arithmetic, body(): return result[None, None]  0.74 us

profile of v6, /device:TPU:199, one launch (start us, length us, event | category | flops | bytes accessed | tf_op | source)
XLA Modules:
  0.0 22.0 jit_solution(16309748840344068394)
XLA Ops:
  0.0 21.2 %shard_map.55 = (f32[4,128,128]{2,1,0:T(8,128)S(1)}, bf16[2,4,128,128]{3,2,1,0:T(8,128)(2,1)S(1)}) custom-call(s32[2,4,12]{2,1,0:T(4,128)} %a_cols_hbm.1, s32[2,4,12]{2,1,0:T(4,128)} %slot_map_hbm.1, s32[2,4]{1,0:T(2,128)} %aggregate_hbm.1, bf16[96,128,128]{2,1,0:T(8,128)(2,1)} %bitcast.9, bf16[2,4,128,128]{3,2,1,0:T(8,128)(2,1)} %p_hbm.1), custom_call_target="tpu_custom_call" | custom-call | tf_op jit(solution)/shard_map/pallas_call | solution.py:362
  21.2 0.7 %fusion = f32[1,1,4,128,128]{4,3,2,1,0:T(8,128)} fusion(f32[4,128,128]{2,1,0:T(8,128)S(1)} %get-tuple-element.7, bf16[2,4,128,128]{3,2,1,0:T(8,128)(2,1)S(1)} %get-tuple-element.8), kind=kLoop, calls=%fused_computation.1 | loop fusion | flops 262144 | bytes 786432 | tf_op jit(solution)/shard_map/broadcast_in_dim | solution.py:407

commit v7 on v6

--- a/solution.py
+++ b/solution.py
@@ -11,6 +11,7 @@
 SIDES = 3
 ROWS = 6
 NEAR = 6 * ROWS
+RING = 8
 GROUPS = (4, 2, 2)
 MESH = pl.DeviceIdType.MESH
 F32 = jnp.float32
@@ -63,10 +64,15 @@
             )
         )
 
-    is_relay, is_source = (dom == 0) & (col == 1), (dom == 1) & (col == 0)
-    tell(barrier, (dom + 1, col), has_up, dom > 0)
+    is_corner, is_relay, is_source = (dom == 0) & (col == 0), (dom == 0) & (col == 1), (dom == 1) & (col == 0)
+    turn = lax.rem(dom, RING)
+    late_below, late_above = (dom == 1) | (has_up & (turn == RING - 1)), has_up & (turn == 3)
+    replies_up = (dom == 0) | ((dom < n_dom - 2) & (turn == RING - 2))
+    replies_down = has_down & (turn == 4)
+    early_below, early_above = has_down & jnp.logical_not(late_below), has_up & jnp.logical_not(late_above)
+    tell(barrier, (dom + 1, col), has_up, jnp.logical_not(replies_up))
     tell(barrier, (dom + 1, inner), is_relay)
-    tell(barrier, (dom - 1, col), has_down)
+    tell(barrier, (dom - 1, col), has_down, jnp.logical_not(replies_down))
     tell(barrier, (dom, inner), col > 0)
     tell(barrier, (dom, outer), has_outer, is_second)
     own_p = [
@@ -86,9 +92,10 @@
     for copy in small:
         copy.start()
 
-    heard = (dom > 1, has_up, col != 1, has_outer & is_first, is_source)
+    heard = (early_below, early_above, col != 1, has_outer & is_first, is_source)
     pl.semaphore_wait(barrier, sum(condition.astype(jnp.int32) for condition in heard))
-    tell(ready.at[0], (dom + 1, col), dom == 0, col > 0)
+    tell(ready.at[0], (dom + 1, col), replies_up, jnp.logical_not(is_corner))
+    tell(ready.at[3], (dom - 1, col), replies_down)
     tell(ready.at[1], (dom, inner), col == 0)
     tell(ready.at[2], (dom, outer), has_outer, is_first)
 
@@ -152,15 +159,9 @@
     partners = (has_outer, has_outer, None, None)
     at_once = ((has_outer & is_first,) * 2) + ((col != 1,) * 2)
     for part in range(4):
-        given(has_up)(by_row[part][0].start)
-        given(dom > 1)(by_row[part][1].start)
+        given(early_above)(by_row[part][0].start)
+        given(early_below)(by_row[part][1].start)
         given(at_once[part])(by_col[part][1].start)
-
-    @pl.when((dom == 1) & (col > 0))
-    def _():
-        pl.semaphore_wait(ready.at[0], 1)
-        for part in range(4):
-            by_row[part][1].start()
 
     @pl.when(is_source)
     def _():
@@ -232,6 +233,18 @@
     for t in members[0]:
         tabulate(t)
 
+    @pl.when(late_below & jnp.logical_not(is_source))
+    def _():
+        pl.semaphore_wait(ready.at[0], 1)
+        for part in range(4):
+            by_row[part][1].start()
+
+    @pl.when(late_above)
+    def _():
+        pl.semaphore_wait(ready.at[3], 1)
+        for part in range(4):
+            by_row[part][0].start()
+
     @pl.when(has_outer & is_second)
     def _():
         pl.semaphore_wait(ready.at[2], 1)
@@ -313,43 +326,41 @@
         if i > 0:
             coarse_sums(i - 1, group_of[i - 1])
 
-    def of_side(side):
+    def of_side(side, j):
+        lanes = pl.ds(j * tile, tile)
         value = None
         for group in range(3):
             at = group * (SIDES + 1) + side
-            part = totals[group][side_ends[at + 1]] - totals[group][side_ends[at]]
+            part = totals[group][side_ends[at + 1], :, lanes] - totals[group][side_ends[at], :, lanes]
             value = part if value is None else value + part
         return value
 
-    leave = []
     kept = pltpu.make_async_copy(away.at[0], arrived.at[0], own_sem.at[2])
     for partner in range(2):
         side = (2 * core, 2 - 2 * core)[partner]
-        value = of_side(side).astype(BF16)
         for j in range(CSLOTS):
-            away[partner, j] = value[:, j * tile:(j + 1) * tile]
-        copy = pltpu.make_async_remote_copy(
-            src_ref=away.at[partner],
-            dst_ref=arrived.at[partner],
-            send_sem=away_send.at[partner],
-            recv_sem=away_recv.at[partner],
-            device_id=(dom, (outer, inner)[partner]),
-            device_id_type=MESH,
-        )
-        given((has_outer, None)[partner])(copy.start)
-        leave.append(copy)
+            away[partner, j] = of_side(side, j).astype(BF16)
+            copy = pltpu.make_async_remote_copy(
+                src_ref=away.at[partner, j],
+                dst_ref=arrived.at[partner, j],
+                send_sem=away_send.at[partner],
+                recv_sem=away_recv.at[partner],
+                device_id=(dom, (outer, inner)[partner]),
+                device_id_type=MESH,
+            )
+            given((has_outer, None)[partner])(copy.start)
     given(jnp.logical_not(has_outer))(kept.start)
-    value = of_side(1)
     for j in range(CSLOTS):
-        here[j] = value[:, j * tile:(j + 1) * tile]
+        here[j] = of_side(1, j)
 
     for way in range(2):
         given(takes[way])(functools.partial(arrive, row_send.at[way], tiles))
     given(is_relay)(functools.partial(arrive, relay_send, tiles))
     arrive_pieces(col_send.at[0], 4, has_outer)
     arrive_pieces(col_send.at[1], 4)
-    leave[1].wait()
-    given(has_outer)(leave[0].wait)
+    for partner in (1, 0):
+        for semaphore in (away_send, away_recv):
+            given((has_outer, None)[partner])(functools.partial(arrive, semaphore.at[partner], CSLOTS))
     given(jnp.logical_not(has_outer))(kept.wait)
 
 
@@ -387,7 +398,7 @@
             pltpu.SMEM((tiles * (CSLOTS + 1),), jnp.int32),
             pltpu.SMEM((tiles,), jnp.int32),
             pltpu.SMEM((3 * (SIDES + 1),), jnp.int32),
-            pltpu.SemaphoreType.REGULAR((3,)),
+            pltpu.SemaphoreType.REGULAR((4,)),
             pltpu.SemaphoreType.DMA,
             pltpu.SemaphoreType.DMA,
             pltpu.SemaphoreType.DMA((3,)),

time: 22.1 us -> 22.1 us (level)
  no operation moved by 1% of the time
where the time goes in v7:
time: 22.1 us; the launch traced here: 21.9 us
  Pallas kernels  21.2 us (96%)
  other arithmetic  0.74 us (3%)
    pallas_call x1, Pallas kernels, body(): pl.pallas_call(functools.partial(kernel, n_dom, n_col), out_shape=(pltpu....  21.2 us
    broadcast_in_dim x1, other arithmetic, body(): return result[None, None]  0.74 us

profile of v7, /device:TPU:199, one launch (start us, length us, event | category | flops | bytes accessed | tf_op | source)
XLA Modules:
  0.0 21.9 jit_solution(594718228619037885)
XLA Ops:
  0.0 21.2 %shard_map.55 = (f32[4,128,128]{2,1,0:T(8,128)S(1)}, bf16[2,4,128,128]{3,2,1,0:T(8,128)(2,1)S(1)}) custom-call(s32[2,4,12]{2,1,0:T(4,128)} %a_cols_hbm.1, s32[2,4,12]{2,1,0:T(4,128)} %slot_map_hbm.1, s32[2,4]{1,0:T(2,128)} %aggregate_hbm.1, bf16[96,128,128]{2,1,0:T(8,128)(2,1)} %bitcast.9, bf16[2,4,128,128]{3,2,1,0:T(8,128)(2,1)} %p_hbm.1), custom_call_target="tpu_custom_call" | custom-call | tf_op jit(solution)/shard_map/pallas_call | solution.py:373
  21.2 0.7 %fusion = f32[1,1,4,128,128]{4,3,2,1,0:T(8,128)} fusion(f32[4,128,128]{2,1,0:T(8,128)S(1)} %get-tuple-element.7, bf16[2,4,128,128]{3,2,1,0:T(8,128)(2,1)S(1)} %get-tuple-element.8), kind=kLoop, calls=%fused_computation.1 | loop fusion | flops 262144 | bytes 786432 | tf_op jit(solution)/shard_map/broadcast_in_dim | solution.py:418
